TPU v7x, 128 devices: a whole 4x4x4 slice. The times are simulated.
128 devices in a mesh: expert: 32 (over x, y, core), dp: 4 (over z).
Axes of the slice: x: 4, y: 4, z: 4, core: 2. Of those that a mesh axis runs over, the one named last changes fastest.
Arguments:
- tokens: bfloat16 [32768, 2048], P(('expert', 'dp')), may hold values from -6 to 6
- grad_out: bfloat16 [32768, 2048], P(('expert', 'dp')), may hold values from -6 to 6
- routes: int32 [32768, 2], P(('expert', 'dp')), may hold values from 0 to 31, all different within a row; in each aligned block of 256 rows (0 to 255, 256 to 511, ...) at most 32 rows name the same one
- gate_probs: bfloat16 [32768, 2], P(('expert', 'dp')), may hold values from 0.099609375 to 1
- w_gate: bfloat16 [32, 768, 2048], P('expert'), may hold values from -0.125 to 0.125
- w_up: bfloat16 [32, 768, 2048], P('expert'), may hold values from -0.125 to 0.125
- w_down: bfloat16 [32, 768, 2048], P('expert'), may hold values from -0.21875 to 0.21875
Outputs:
- d_tokens: bfloat16 [32768, 2048], P(('expert', 'dp'))
- d_probs: float32 [32768, 2], P(('expert', 'dp'))
- grad_w_gate: float32 [32, 768, 2048], P('expert', 'dp')
- grad_w_up: float32 [32, 768, 2048], P('expert', 'dp')
- grad_w_down: float32 [32, 768, 2048], P('expert', 'dp')
Inputs may be any that keep to these rules, and one draw needn't show every extreme that they name: `routes`: within the 256 rows of one device (aligned blocks), each expert is named at most 32 times, a bound that some block reaches; the two experts of a row differ.
All inputs are finite; a program needn't handle non-finite values.
Results may differ from a plain program's by a relative error of at most 0.0049.
Values may be sent and summed in bfloat16 or wider, within the bound.
A program may use at most 192 MiB of HBM per device.

v0:
```python
import jax
import jax.numpy as jnp
from jax import lax
from jax.sharding import PartitionSpec as P


def forward_part(x_rows, dy_rows, p_rows, w_g, w_u, w_d):
    contract_d = (((1,), (1,)), ((), ()))
    gate_pre = lax.dot_general(x_rows, w_g, contract_d, preferred_element_type=jnp.float32)
    upward = lax.dot_general(x_rows, w_u, contract_d, preferred_element_type=jnp.float32)
    sig_gate = jax.nn.sigmoid(gate_pre)
    active = gate_pre * sig_gate * upward
    scaled = (p_rows.astype(jnp.float32)[:, None] * dy_rows.astype(jnp.float32)).astype(
        jnp.bfloat16
    )
    contract_rows = (((0,), (0,)), ((), ()))
    grad_down = lax.dot_general(
        active.astype(jnp.bfloat16), scaled, contract_rows, preferred_element_type=jnp.float32
    )
    back_act = lax.dot_general(dy_rows, w_d, contract_d, preferred_element_type=jnp.float32)
    d_prob = jnp.sum(active * back_act, axis=1)
    return (gate_pre, upward, sig_gate, back_act, grad_down, d_prob)


def inner_part(x_rows, p_rows, gate_pre, upward, sig_gate, back_act, w_g, w_u):
    scaled_back = p_rows.astype(jnp.float32)[:, None] * back_act
    d_gate = (scaled_back * upward * (sig_gate + gate_pre * sig_gate * (1.0 - sig_gate))).astype(
        jnp.bfloat16
    )
    d_up = (scaled_back * gate_pre * sig_gate).astype(jnp.bfloat16)
    contract_rows = (((0,), (0,)), ((), ()))
    grad_gate = lax.dot_general(d_gate, x_rows, contract_rows, preferred_element_type=jnp.float32)
    grad_up = lax.dot_general(d_up, x_rows, contract_rows, preferred_element_type=jnp.float32)
    d_input = jnp.dot(d_gate, w_g, preferred_element_type=jnp.float32) + jnp.dot(
        d_up, w_u, preferred_element_type=jnp.float32
    )
    return (grad_gate, grad_up, d_input)


def per_device(tokens, grad_out, routes, gate_probs, w_gate, w_up, w_down):
    tok_count = tokens.shape[0]
    model_width = tokens.shape[1]
    n_expert = lax.axis_size("expert")
    capacity = 4 * tok_count // n_expert
    n_assign = 2 * tok_count
    row_total = n_expert * capacity
    flat_route = routes.reshape(-1)
    onehot = (flat_route[:, None] == jnp.arange(n_expert, dtype=jnp.int32)[None, :]).astype(
        jnp.int32
    )
    slot_rank = jnp.sum(jnp.cumsum(onehot, axis=0) * onehot, axis=1) - 1
    target = flat_route * capacity + slot_rank
    source_of = (
        jnp.full((row_total,), n_assign, jnp.int32)
        .at[target]
        .set(jnp.arange(n_assign, dtype=jnp.int32))
    )
    token_of = source_of // 2
    zero_row = jnp.zeros((1, model_width), jnp.bfloat16)
    x_send = jnp.concatenate([tokens, zero_row], axis=0)[token_of].reshape(
        n_expert, capacity, model_width
    )
    dy_send = jnp.concatenate([grad_out, zero_row], axis=0)[token_of].reshape(
        n_expert, capacity, model_width
    )
    p_send = jnp.concatenate([gate_probs.reshape(-1), jnp.zeros((1,), jnp.bfloat16)], axis=0)[
        source_of
    ].reshape(n_expert, capacity)
    x_recv, dy_recv, p_recv = (
        lax.all_to_all(x_send, "expert", split_axis=0, concat_axis=0, tiled=True),
        lax.all_to_all(dy_send, "expert", split_axis=0, concat_axis=0, tiled=True),
        lax.all_to_all(p_send, "expert", split_axis=0, concat_axis=0, tiled=True),
    )
    x_rows = x_recv.reshape(row_total, model_width)
    dy_rows = dy_recv.reshape(row_total, model_width)
    p_rows = p_recv.reshape(row_total)
    w_g = w_gate[0]
    w_u = w_up[0]
    w_d = w_down[0]
    gate_pre, upward, sig_gate, back_act, grad_down, dprob_rows = forward_part(
        x_rows, dy_rows, p_rows, w_g, w_u, w_d
    )
    grad_gate, grad_up, d_rows = inner_part(
        x_rows, p_rows, gate_pre, upward, sig_gate, back_act, w_g, w_u
    )
    grad_g, grad_u, grad_d = (
        lax.psum_scatter(grad_gate, "dp", scatter_dimension=0, tiled=True),
        lax.psum_scatter(grad_up, "dp", scatter_dimension=0, tiled=True),
        lax.psum_scatter(grad_down, "dp", scatter_dimension=0, tiled=True),
    )
    dx_back, dp_back = (
        lax.all_to_all(
            d_rows.reshape(n_expert, capacity, model_width),
            "expert",
            split_axis=0,
            concat_axis=0,
            tiled=True,
        ),
        lax.all_to_all(
            dprob_rows.reshape(n_expert, capacity),
            "expert",
            split_axis=0,
            concat_axis=0,
            tiled=True,
        ),
    )
    per_assign = dx_back.reshape(row_total, model_width)[target].reshape(tok_count, 2, model_width)
    d_tokens = (per_assign[:, 0] + per_assign[:, 1]).astype(jnp.bfloat16)
    d_probs = dp_back.reshape(-1)[target].reshape(tok_count, 2)
    return (d_tokens, d_probs, grad_g[None], grad_u[None], grad_d[None])


def solution(mesh):
    placed = (
        P(("expert", "dp"), None),
        P(("expert", "dp"), None),
        P(("expert", "dp"), None),
        P(("expert", "dp"), None),
        P("expert", None, None),
        P("expert", None, None),
        P("expert", None, None),
    )
    return jax.shard_map(
        per_device,
        mesh=mesh,
        in_specs=placed,
        out_specs=(
            P(("expert", "dp"), None),
            P(("expert", "dp"), None),
            P("expert", "dp", None),
            P("expert", "dp", None),
            P("expert", "dp", None),
        ),
        check_vma=False,
    )
```

profile of v0, /device:TPU:104, one launch (start us, length us, event | category | flops | bytes accessed | tf_op | source)
XLA Modules:
  0.0 382.9 jit_solution(10080245607272934092)
XLA Ops:
  7.2 0.8 broadcast_multiply_fusion
  8.0 0.9 copy.24
  9.2 0.8 copy.22
  10.5 1.2 reduce-window.6
  12.1 2.4 scatter_custom_fusion
  14.6 6.8 %gather_fusion = bf16[1024]{0:T(1024)(128)(2,1)S(1)} fusion(bf16[513]{0:T(1024)(128)(2,1)S(1)} %pad_maximum_fusion, s32[1024]{0:T(1024)S(1)} %get-tuple-element.20), kind=kCustom, calls=%fused_computation | custom fusion | bytes 8192 | tf_op jit(solution)/shard_map/gather | solution.py:66
  22.1 7.5 %all-to-all-start = ((bf16[32,1,32]{2,1,0:T(2,128)(2,1)}), bf16[32,1,32]{2,1,0:T(2,128)(2,1)S(1)}, u32[]{:S(2)}, u32[]{:S(2)}) async-start(bf16[32,1,32]{2,1,0:T(2,128)(2,1)} %all_to_all.28), calls=%async_computation | async-start | bytes 32768 | tf_op jit(solution)/shard_map/all_to_all | solution.py:72
  29.6 2.3 concatenate.11
  31.9 10.2 %gather_fusion.2 = bf16[1024,2048]{1,0:T(8,128)(2,1)} fusion(bf16[257,2048]{1,0:T(8,128)(2,1)} %concatenate.11, s32[1024]{0:T(1024)S(1)} %get-tuple-element.21), kind=kCustom, calls=%fused_computation.2 | custom fusion | bytes 8392704 | tf_op jit(solution)/shard_map/gather | solution.py:60
  42.2 7.4 %all-to-all-start.2 = ((bf16[32,32,2048]{2,1,0:T(8,128)(2,1)}), bf16[32,32,2048]{2,1,0:T(8,128)(2,1)}, u32[]{:S(2)}, u32[]{:S(2)}) async-start(bf16[32,32,2048]{2,1,0:T(8,128)(2,1)} %bitcast.54), calls=%async_computation.2 | async-start | bytes 8388608 | tf_op jit(solution)/shard_map/all_to_all | solution.py:70
  49.6 2.3 concatenate.10
  51.9 10.2 %gather_fusion.1 = bf16[1024,2048]{1,0:T(8,128)(2,1)} fusion(bf16[257,2048]{1,0:T(8,128)(2,1)} %concatenate.10, s32[1024]{0:T(1024)S(1)} %get-tuple-element.21), kind=kCustom, calls=%fused_computation.1 | custom fusion | bytes 8392704 | tf_op jit(solution)/shard_map/gather | solution.py:63
  62.1 42.0 %all-to-all-done.2 = bf16[32,32,2048]{2,1,0:T(8,128)(2,1)} async-done(((bf16[32,32,2048]{2,1,0:T(8,128)(2,1)}), bf16[32,32,2048]{2,1,0:T(8,128)(2,1)}, u32[]{:S(2)}, u32[]{:S(2)}) %all-to-all-start.2) | async-done | bytes 4194336 | tf_op jit(solution)/shard_map/all_to_all | solution.py:70
  104.1 4.8 %all-to-all-start.1 = ((bf16[32,32,2048]{2,1,0:T(8,128)(2,1)}), bf16[32,32,2048]{2,1,0:T(8,128)(2,1)}, u32[]{:S(2)}, u32[]{:S(2)}) async-start(bf16[32,32,2048]{2,1,0:T(8,128)(2,1)} %bitcast.53), calls=%async_computation.1 | async-start | bytes 8388608 | tf_op jit(solution)/shard_map/all_to_all | solution.py:71
  109.5 7.5 %fusion.4 = f32[1024,768]{0,1:T(8,128)} fusion(bf16[1024,2048]{1,0:T(8,128)(2,1)} %bitcast.7, bf16[1,768,2048]{2,1,0:T(8,128)(2,1)S(1)} %copy-done), kind=kOutput, calls=%fused_computation.12 | convolution fusion | flops 3221225472 | bytes 10485760 | tf_op jit(solution)/shard_map/dot_general | solution.py:9
  117.0 7.4 %fusion.7 = f32[1024,768]{0,1:T(8,128)} fusion(bf16[1024,2048]{1,0:T(8,128)(2,1)} %bitcast.7, bf16[1,768,2048]{2,1,0:T(8,128)(2,1)S(1)} %copy-done.1), kind=kOutput, calls=%fused_computation.15 | convolution fusion | flops 3221225472 | bytes 10485760 | tf_op jit(solution)/shard_map/dot_general | solution.py:10
  124.3 39.2 %all-to-all-done.1 = bf16[32,32,2048]{2,1,0:T(8,128)(2,1)} async-done(((bf16[32,32,2048]{2,1,0:T(8,128)(2,1)}), bf16[32,32,2048]{2,1,0:T(8,128)(2,1)}, u32[]{:S(2)}, u32[]{:S(2)}) %all-to-all-start.1) | async-done | bytes 4194336 | tf_op jit(solution)/shard_map/all_to_all | solution.py:71
  163.5 10.3 %fusion = f32[768,2048]{1,0:T(8,128)} fusion(bf16[1024,2048]{1,0:T(8,128)(2,1)} %bitcast.4, f32[1024]{0:T(1024)S(1)} %reshape.122, f32[1024,768]{0,1:T(8,128)} %fusion.7, f32[1024,768]{0,1:T(8,128)} %fusion.4), kind=kOutput, calls=%fused_computation.7 | convolution fusion | flops 3232235520 | bytes 16781312 | tf_op jit(solution)/shard_map/dot_general | solution.py:17
  174.4 10.9 %multiply_reduce_fusion = (f32[1024]{0:T(1024)S(1)}, bf16[1024,768]{0,1:T(8,128)(2,1)S(1)}, bf16[1024,768]{0,1:T(8,128)(2,1)}) fusion(f32[1024,768]{0,1:T(8,128)} %fusion.7, f32[1024,768]{0,1:T(8,128)} %fusion.4, f32[1024]{0:T(1024)S(1)} %reshape.122, bf16[1024,2048]{1,0:T(8,128)(2,1)} %bitcast.4, bf16[1,768,2048]{2,1,0:T(8,128)(2,1)} %param.13), kind=kOutput, calls=%fused_computation.19 | convolution fusion | flops 3234593792 | bytes 16785408 | tf_op jit(solution)/shard_map/dot_general | solution.py:20
  185.3 1.2 copy-done.4
  186.5 7.5 %fusion.27 = f32[768,2048]{1,0:T(8,128)} fusion(bf16[1024,768]{0,1:T(8,128)(2,1)S(1)} %get-tuple-element.16, bf16[1024,2048]{1,0:T(8,128)(2,1)} %bitcast.7), kind=kOutput, calls=%fused_computation.57 | convolution fusion | flops 3221225472 | bytes 12058624 | tf_op jit(solution)/shard_map/dot_general | solution.py:32
  194.0 8.7 %fusion.28 = f32[768,2048]{1,0:T(8,128)} fusion(bf16[1024,768]{0,1:T(8,128)(2,1)} %get-tuple-element.17, bf16[1024,2048]{1,0:T(8,128)(2,1)} %bitcast.7), kind=kOutput, calls=%fused_computation.58 | convolution fusion | flops 3221225472 | bytes 12058624 | tf_op jit(solution)/shard_map/dot_general | solution.py:33
  203.5 5.1 %all-to-all-start.4 = ((f32[32,1,32]{2,1,0:T(1,128)}), f32[32,1,32]{2,1,0:T(1,128)S(1)}, u32[]{:S(2)}, u32[]{:S(2)}) async-start(f32[32,1,32]{2,1,0:T(1,128)} %all_to_all.26), calls=%async_computation.4 | async-start | bytes 32768 | tf_op jit(solution)/shard_map/all_to_all | solution.py:99
  208.6 5.1 %fusion.2 = f32[1024,2048]{1,0:T(8,128)S(1)} fusion(bf16[1024,768]{0,1:T(8,128)(2,1)} %copy-done.4, bf16[1,768,2048]{2,1,0:T(8,128)(2,1)S(1)} %copy-done), kind=kOutput, calls=%fused_computation.10 | convolution fusion | flops 3221225472 | bytes 13107200 | tf_op jit(solution)/shard_map/dot_general | solution.py:34
  213.8 5.9 %convolution_add_fusion = f32[1024,2048]{1,0:T(8,128)} fusion(f32[1024,2048]{1,0:T(8,128)S(1)} %fusion.2, bf16[1024,768]{0,1:T(8,128)(2,1)S(1)} %copy-done.3, bf16[1,768,2048]{2,1,0:T(8,128)(2,1)S(1)} %copy-done.2), kind=kOutput, calls=%fused_computation.9 | convolution fusion | flops 3223322624 | bytes 21495808 | tf_op jit(solution)/shard_map/dot_general | solution.py:34
  219.7 7.8 %all-to-all-start.3 = ((f32[32,32,2048]{2,1,0:T(8,128)}), f32[32,32,2048]{2,1,0:T(8,128)}, u32[]{:S(2)}, u32[]{:S(2)}) async-start(f32[32,32,2048]{2,1,0:T(8,128)} %bitcast.55), calls=%async_computation.3 | async-start | bytes 16777216 | tf_op jit(solution)/shard_map/all_to_all | solution.py:92
  228.8 2.3 gather_fusion.4
  231.9 119.5 %all-to-all-done.3 = f32[32,32,2048]{2,1,0:T(8,128)} async-done(((f32[32,32,2048]{2,1,0:T(8,128)}), f32[32,32,2048]{2,1,0:T(8,128)}, u32[]{:S(2)}, u32[]{:S(2)}) %all-to-all-start.3) | async-done | bytes 8388640 | tf_op jit(solution)/shard_map/all_to_all | solution.py:92
  351.4 8.8 %gather_fusion.3 = f32[512,2048]{1,0:T(8,128)} fusion(f32[1024,2048]{1,0:T(8,128)} %bitcast.11, s32[1024]{0:T(1024)S(1)} %pad_clamp_fusion), kind=kCustom, calls=%fused_computation.3 | custom fusion | bytes 8390656 | tf_op jit(solution)/shard_map/gather | solution.py:107
  360.2 5.9 %reshape.119 = f32[256,2,2048]{2,1,0:T(2,128)} reshape(f32[512,2048]{1,0:T(8,128)} %gather_fusion.3) | data formatting | bytes 8388608 | tf_op jit(solution)/shard_map/reshape | solution.py:107
  366.1 7.9 %fusion.26 = (f32[256,1,2048]{2,1,0:T(1,128)S(1)}, f32[256,1,2048]{2,1,0:T(1,128)S(1)}) fusion(f32[256,2,2048]{2,1,0:T(2,128)} %reshape.119), kind=kLoop, calls=%fused_computation.56 | loop fusion | bytes 8388608 | tf_op jit(solution)/shard_map/slice | solution.py:108
  374.0 2.1 fusion.15
  (45 shorter events, 5.7 us)
Async XLA Ops:
  7.2 102.3 %copy-start = (bf16[1,768,2048]{2,1,0:T(8,128)(2,1)S(1)}, bf16[1,768,2048]{2,1,0:T(8,128)(2,1)}, u32[]{:S(2)}) copy-start(bf16[1,768,2048]{2,1,0:T(8,128)(2,1)} %param.11) | copy-start | bytes 9437188
  22.1 20.1 %all-to-all-start = ((bf16[32,1,32]{2,1,0:T(2,128)(2,1)}), bf16[32,1,32]{2,1,0:T(2,128)(2,1)S(1)}, u32[]{:S(2)}, u32[]{:S(2)}) async-start(bf16[32,1,32]{2,1,0:T(2,128)(2,1)} %all_to_all.28), calls=%async_computation | async-start | bytes 32768 | tf_op jit(solution)/shard_map/all_to_all | solution.py:72
  42.2 62.0 %all-to-all-start.2 = ((bf16[32,32,2048]{2,1,0:T(8,128)(2,1)}), bf16[32,32,2048]{2,1,0:T(8,128)(2,1)}, u32[]{:S(2)}, u32[]{:S(2)}) async-start(bf16[32,32,2048]{2,1,0:T(8,128)(2,1)} %bitcast.54), calls=%async_computation.2 | async-start | bytes 8388608 | tf_op jit(solution)/shard_map/all_to_all | solution.py:70
  104.1 59.4 %all-to-all-start.1 = ((bf16[32,32,2048]{2,1,0:T(8,128)(2,1)}), bf16[32,32,2048]{2,1,0:T(8,128)(2,1)}, u32[]{:S(2)}, u32[]{:S(2)}) async-start(bf16[32,32,2048]{2,1,0:T(8,128)(2,1)} %bitcast.53), calls=%async_computation.1 | async-start | bytes 8388608 | tf_op jit(solution)/shard_map/all_to_all | solution.py:71
  109.0 267.1 %reduce-scatter.8.cloned.1.call-start = ((), (), s32[]{:S(2)}) async-start(), calls=%async_computation.10 | async-start | bytes 7864320 | tf_op jit(solution)/shard_map/reduce_scatter | solution.py:89
  109.5 7.5 %copy-start.1 = (bf16[1,768,2048]{2,1,0:T(8,128)(2,1)S(1)}, bf16[1,768,2048]{2,1,0:T(8,128)(2,1)}, u32[]{:S(2)}) copy-start(bf16[1,768,2048]{2,1,0:T(8,128)(2,1)} %param.12) | copy-start | bytes 9437188
  173.9 202.2 %reduce-scatter.4.cloned.1.call-start = ((), (), s32[]{:S(2)}) async-start(), calls=%async_computation.8 | async-start | bytes 7864320 | tf_op jit(solution)/shard_map/reduce_scatter | solution.py:87
  185.3 1.2 copy-start.4
  194.0 182.1 %reduce-scatter.6.cloned.1.call-start = ((), (), s32[]{:S(2)}) async-start(), calls=%async_computation.9 | async-start | bytes 7864320 | tf_op jit(solution)/shard_map/reduce_scatter | solution.py:88
  203.5 16.2 %all-to-all-start.4 = ((f32[32,1,32]{2,1,0:T(1,128)}), f32[32,1,32]{2,1,0:T(1,128)S(1)}, u32[]{:S(2)}, u32[]{:S(2)}) async-start(f32[32,1,32]{2,1,0:T(1,128)} %all_to_all.26), calls=%async_computation.4 | async-start | bytes 32768 | tf_op jit(solution)/shard_map/all_to_all | solution.py:99
  208.6 5.2 %copy-start.2 = (bf16[1,768,2048]{2,1,0:T(8,128)(2,1)S(1)}, bf16[1,768,2048]{2,1,0:T(8,128)(2,1)}, u32[]{:S(2)}) copy-start(bf16[1,768,2048]{2,1,0:T(8,128)(2,1)} %param.12) | copy-start | bytes 9437188
  208.6 5.1 %copy-start.3 = (bf16[1024,768]{0,1:T(8,128)(2,1)S(1)}, bf16[1024,768]{0,1:T(8,128)(2,1)}, u32[]{:S(2)}) copy-start(bf16[1024,768]{0,1:T(8,128)(2,1)} %get-tuple-element.17) | copy-start | bytes 4718596
  219.7 131.8 %all-to-all-start.3 = ((f32[32,32,2048]{2,1,0:T(8,128)}), f32[32,32,2048]{2,1,0:T(8,128)}, u32[]{:S(2)}, u32[]{:S(2)}) async-start(f32[32,32,2048]{2,1,0:T(8,128)} %bitcast.55), calls=%async_computation.3 | async-start | bytes 16777216 | tf_op jit(solution)/shard_map/all_to_all | solution.py:92
Sparse Core Ops, SparseCore 0:
  174.0 60.4 reduce-scatter.7
  237.5 63.7 reduce-scatter.3
  304.2 63.7 reduce-scatter.5
where the time goes:
time: 389 us; the launch traced here: 383 us
  waiting for transfers between devices  201 us (52%)
  local copies, waits for them, and re-layouts  65.9 us (17%)
  matrix products  63.2 us (16%)
  starting transfers between devices  33.7 us (9%)
  between operations  14.2 us (4%)
  other arithmetic  5.03 us (1%)
    all_to_all x1, waiting for transfers between devices, per_device(): lax.all_to_all(d_rows.reshape(n_expert, capacity, model_width), 'expert',...  120 us
    all_to_all x1, waiting for transfers between devices, per_device(): lax.all_to_all(x_send, 'expert', split_axis=0, concat_axis=0, tiled=True)  42 us
    all_to_all x1, waiting for transfers between devices, per_device(): lax.all_to_all(dy_send, 'expert', split_axis=0, concat_axis=0, tiled=True)  39.2 us
    dot_general x1, matrix products, forward_part(): lax.dot_general(dy_rows, w_d, contract_d, preferred_element_type=jnp.floa...  10.9 us
    dot_general x1, matrix products, forward_part(): lax.dot_general(active.astype(jnp.bfloat16), scaled, contract_rows, prefe...  10.3 us
    gather x1, local copies, waits for them, and re-layouts, per_device(): jnp.concatenate([tokens, zero_row], axis=0)[token_of]  10.2 us
    gather x1, local copies, waits for them, and re-layouts, per_device(): jnp.concatenate([grad_out, zero_row], axis=0)[token_of]  10.2 us
    gather x1, local copies, waits for them, and re-layouts, per_device(): dx_back.reshape(row_total, model_width)[target]  8.76 us
  transfers between devices with their start and end apart: 8, of which 3 were waited for; matrix products, arithmetic and copies ran while one was open for 28% of the time, Pallas kernels for 0%

commit v1 on v0

v1 whole, which is shorter than its diff:
```python
import jax
import jax.numpy as jnp
from jax import lax
from jax.sharding import PartitionSpec as P

F32 = jnp.float32
BF16 = jnp.bfloat16
CONTRACT_D = (((1,), (1,)), ((), ()))
CONTRACT_ROWS = (((0,), (0,)), ((), ()))


def per_device(tokens, grad_out, routes, gate_probs, w_gate, w_up, w_down):
    tok_count, model_width = tokens.shape
    n_expert = lax.axis_size("expert")
    capacity = 4 * tok_count // n_expert
    row_total = n_expert * capacity

    def swap(a):
        return lax.all_to_all(a, "expert", split_axis=0, concat_axis=0, tiled=True)

    experts = jnp.arange(n_expert, dtype=jnp.int32)
    hot = [(routes[:, k][None, :] == experts[:, None]) for k in range(2)]
    before = (
        jnp.arange(tok_count)[:, None] < jnp.arange(tok_count)[None, :]
    ).astype(BF16)
    ranks = [jnp.dot(h.astype(BF16), before, preferred_element_type=F32) for h in hot]
    ranks[1] = ranks[1] + jnp.sum(hot[0].astype(F32), axis=1, keepdims=True)
    base = (experts * capacity)[:, None]
    target = [
        jnp.sum(jnp.where(h, r.astype(jnp.int32) + base, 0), axis=0)
        for h, r in zip(hot, ranks)
    ]
    slots = jnp.arange(row_total, dtype=jnp.int32)
    pick = [slots[:, None] == t[None, :] for t in target]
    probs = gate_probs.astype(F32)
    take = jnp.where(pick[0] | pick[1], 1.0, 0.0).astype(BF16)
    take_scaled = (
        jnp.where(pick[0], probs[:, 0][None, :], 0.0)
        + jnp.where(pick[1], probs[:, 1][None, :], 0.0)
    ).astype(BF16)
    x_send = jnp.dot(take, tokens, preferred_element_type=F32).astype(BF16)
    s_send = jnp.dot(take_scaled, grad_out, preferred_element_type=F32).astype(BF16)
    x_rows = swap(x_send.reshape(n_expert, capacity, model_width)).reshape(
        row_total, model_width
    )
    s_rows = swap(s_send.reshape(n_expert, capacity, model_width)).reshape(
        row_total, model_width
    )
    w_g, w_u, w_d = w_gate[0], w_up[0], w_down[0]

    def dot(a, b, dims):
        return lax.dot_general(a, b, dims, preferred_element_type=F32)

    gate_pre = dot(x_rows, w_g, CONTRACT_D)
    upward = dot(x_rows, w_u, CONTRACT_D)
    scaled_back = dot(s_rows, w_d, CONTRACT_D)
    sig = jax.nn.sigmoid(gate_pre)
    silu = gate_pre * sig
    active = silu * upward
    dprob_rows = jnp.sum(active * scaled_back, axis=1)
    d_gate = (scaled_back * upward * (sig + silu * (1.0 - sig))).astype(BF16)
    d_up = (scaled_back * silu).astype(BF16)

    def reduce_rows(a):
        return lax.psum_scatter(
            a.astype(BF16), "dp", scatter_dimension=0, tiled=True
        ).astype(F32)[None]

    grad_d = reduce_rows(dot(active.astype(BF16), s_rows, CONTRACT_ROWS))
    grad_g = reduce_rows(dot(d_gate, x_rows, CONTRACT_ROWS))
    grad_u = reduce_rows(dot(d_up, x_rows, CONTRACT_ROWS))
    d_rows = (
        jnp.dot(d_gate, w_g, preferred_element_type=F32)
        + jnp.dot(d_up, w_u, preferred_element_type=F32)
    ).astype(BF16)
    dx_back = swap(d_rows.reshape(n_expert, capacity, model_width)).reshape(
        row_total, model_width
    )
    dp_back = swap(dprob_rows.reshape(n_expert, capacity)).reshape(row_total)
    d_tokens = dot(take, dx_back, CONTRACT_ROWS).astype(BF16)
    d_probs = (
        jnp.stack(
            [jnp.sum(jnp.where(m, dp_back[:, None], 0.0), axis=0) for m in pick], axis=1
        )
        / probs
    )
    return (d_tokens, d_probs, grad_g, grad_u, grad_d)


def solution(mesh):
    rows, experts = P(("expert", "dp"), None), P("expert", None, None)
    split = P("expert", "dp", None)
    return jax.shard_map(
        per_device,
        mesh=mesh,
        in_specs=(rows, rows, rows, rows, experts, experts, experts),
        out_specs=(rows, rows, split, split, split),
        check_vma=False,
    )
```

time: 389 us -> 274 us (0.70)
  the two profiles are of different devices: /device:TPU:104 before, /device:TPU:4 now
where the time goes in v1:
time: 274 us; the launch traced here: 272 us
  waiting for transfers between devices  133 us (49%)
  matrix products  80.1 us (29%)
  starting transfers between devices  32.8 us (12%)
  between operations  13.9 us (5%)
  other arithmetic  9.15 us (3%)
  local copies, waits for them, and re-layouts  3.3 us (1%)
    all_to_all x4, waiting for transfers between devices, swap(): return lax.all_to_all(a, 'expert', split_axis=0, concat_axis=0, tiled=True)  131 us
    dot_general x7, matrix products, dot(): return lax.dot_general(a, b, dims, preferred_element_type=F32)  53.4 us
    all_to_all x4, starting transfers between devices, swap(): return lax.all_to_all(a, 'expert', split_axis=0, concat_axis=0, tiled=True)  32 us
    dot_general x1, matrix products, per_device(): jnp.dot(d_up, w_u, preferred_element_type=F32)  10.3 us
    broadcast_in_dim x3, other arithmetic, reduce_rows(): lax.psum_scatter(a.astype(BF16), 'dp', scatter_dimension=0, tiled=True)  7.41 us
    dot_general x1, matrix products, per_device(): jnp.dot(d_gate, w_g, preferred_element_type=F32)  7.22 us
  transfers between devices with their start and end apart: 7, of which 4 were waited for; matrix products, arithmetic and copies ran while one was open for 27% of the time, Pallas kernels for 0%

profile of v1, /device:TPU:4, one launch (start us, length us, event | category | flops | bytes accessed | tf_op | source)
XLA Modules:
  0.0 272.0 jit_solution(16755010436764362622)
XLA Ops:
  7.2 0.9 fusion.41
  8.5 4.4 %convolution_convert_fusion = bf16[1024,2048]{1,0:T(8,128)(2,1)} fusion(bf16[256,2048]{1,0:T(8,128)(2,1)} %param.7, s32[256]{0:T(256)S(1)} %fusion.18, s32[256]{0:T(256)S(1)} %fusion.17), kind=kOutput, calls=%fused_computation.1 | convolution fusion | flops 1077149696 | bytes 5244928 | tf_op jit(solution)/shard_map/dot_general | solution.py:41
  12.9 7.8 %all-to-all-start.1 = ((bf16[32,32,2048]{2,1,0:T(8,128)(2,1)}), bf16[32,32,2048]{2,1,0:T(8,128)(2,1)}, u32[]{:S(2)}, u32[]{:S(2)}) async-start(bf16[32,32,2048]{2,1,0:T(8,128)(2,1)} %bitcast.49), calls=%async_computation.1 | async-start | bytes 8388608 | tf_op jit(solution)/shard_map/all_to_all | solution.py:19
  20.7 4.5 %convolution_convert_fusion.1 = bf16[1024,2048]{1,0:T(8,128)(2,1)} fusion(bf16[256,2048]{1,0:T(8,128)(2,1)} %param.8, f32[256]{0:T(256)S(1)} %bitcast.58, f32[256]{0:T(256)S(1)} %bitcast.57, s32[256]{0:T(256)S(1)} %fusion.18, s32[256]{0:T(256)S(1)} %fusion.17), kind=kOutput, calls=%fused_computation.2 | convolution fusion | flops 1077411840 | bytes 5246976 | tf_op jit(solution)/shard_map/dot_general | solution.py:42
  25.2 46.4 %all-to-all-done.1 = bf16[32,32,2048]{2,1,0:T(8,128)(2,1)} async-done(((bf16[32,32,2048]{2,1,0:T(8,128)(2,1)}), bf16[32,32,2048]{2,1,0:T(8,128)(2,1)}, u32[]{:S(2)}, u32[]{:S(2)}) %all-to-all-start.1) | async-done | bytes 4194336 | tf_op jit(solution)/shard_map/all_to_all | solution.py:19
  71.6 8.5 %all-to-all-start = ((bf16[32,32,2048]{2,1,0:T(8,128)(2,1)}), bf16[32,32,2048]{2,1,0:T(8,128)(2,1)}, u32[]{:S(2)}, u32[]{:S(2)}) async-start(bf16[32,32,2048]{2,1,0:T(8,128)(2,1)} %bitcast.51), calls=%async_computation | async-start | bytes 8388608 | tf_op jit(solution)/shard_map/all_to_all | solution.py:19
  80.1 0.2 reduce-scatter.8.cloned.1.call-start
  80.4 7.5 %fusion.2 = f32[1024,768]{0,1:T(8,128)} fusion(bf16[1024,2048]{1,0:T(8,128)(2,1)} %bitcast.8, bf16[1,768,2048]{2,1,0:T(8,128)(2,1)S(1)} %copy-done), kind=kOutput, calls=%fused_computation.8 | convolution fusion | flops 3221225472 | bytes 10485760 | tf_op jit(solution)/shard_map/dot_general | solution.py:52
  87.8 7.4 %fusion.5 = f32[1024,768]{0,1:T(8,128)} fusion(bf16[1024,2048]{1,0:T(8,128)(2,1)} %bitcast.8, bf16[1,768,2048]{2,1,0:T(8,128)(2,1)S(1)} %copy-done.2), kind=kOutput, calls=%fused_computation.11 | convolution fusion | flops 3221225472 | bytes 10485760 | tf_op jit(solution)/shard_map/dot_general | solution.py:52
  95.2 35.8 %all-to-all-done = bf16[32,32,2048]{2,1,0:T(8,128)(2,1)} async-done(((bf16[32,32,2048]{2,1,0:T(8,128)(2,1)}), bf16[32,32,2048]{2,1,0:T(8,128)(2,1)}, u32[]{:S(2)}, u32[]{:S(2)}) %all-to-all-start) | async-done | bytes 4194336 | tf_op jit(solution)/shard_map/all_to_all | solution.py:19
  131.0 9.2 %convolution_convert_fusion.2 = bf16[768,2048]{1,0:T(8,128)(2,1)} fusion(bf16[1024,2048]{1,0:T(8,128)(2,1)} %bitcast.5, f32[1024,768]{0,1:T(8,128)} %fusion.5, f32[1024,768]{0,1:T(8,128)} %fusion.2), kind=kOutput, calls=%fused_computation.3 | convolution fusion | flops 3227516928 | bytes 13631488 | tf_op jit(solution)/shard_map/dot_general | solution.py:52
  140.2 0.3 reduce-scatter.4.cloned.1.call-start
  140.4 10.7 %multiply_reduce_fusion = (f32[1024]{0:T(1024)S(1)}, bf16[1024,768]{0,1:T(8,128)(2,1)S(1)}, bf16[1024,768]{0,1:T(8,128)(2,1)}) fusion(f32[1024,768]{0,1:T(8,128)} %fusion.5, f32[1024,768]{0,1:T(8,128)} %fusion.2, bf16[1024,2048]{1,0:T(8,128)(2,1)} %bitcast.5, bf16[1,768,2048]{2,1,0:T(8,128)(2,1)} %param.13), kind=kOutput, calls=%fused_computation.15 | convolution fusion | flops 3233020928 | bytes 16781312 | tf_op jit(solution)/shard_map/dot_general | solution.py:52
  151.1 1.1 copy-done.3
  152.3 7.2 %convolution_convert_fusion.4 = bf16[768,2048]{1,0:T(8,128)(2,1)} fusion(bf16[1024,768]{0,1:T(8,128)(2,1)S(1)} %get-tuple-element.8, bf16[1024,2048]{1,0:T(8,128)(2,1)} %bitcast.8), kind=kOutput, calls=%fused_computation.5 | convolution fusion | flops 3222798336 | bytes 8912896 | tf_op jit(solution)/shard_map/dot_general | solution.py:52
  159.5 0.7 all_to_all.18
  160.2 8.3 %all-to-all-start.3 = ((f32[32,1,32]{2,1,0:T(1,128)}), f32[32,1,32]{2,1,0:T(1,128)S(1)}, u32[]{:S(2)}, u32[]{:S(2)}) async-start(f32[32,1,32]{2,1,0:T(1,128)} %all_to_all.18), calls=%async_computation.3 | async-start | bytes 32768 | tf_op jit(solution)/shard_map/all_to_all | solution.py:19
  168.5 0.3 reduce-scatter.6.cloned.1.call-start
  168.8 7.2 %fusion = f32[1024,2048]{1,0:T(8,128)} fusion(bf16[1024,768]{0,1:T(8,128)(2,1)} %copy-done.3, bf16[1,768,2048]{2,1,0:T(8,128)(2,1)S(1)} %copy-done), kind=kOutput, calls=%fused_computation.6 | convolution fusion | flops 3221225472 | bytes 13107200 | tf_op jit(solution)/shard_map/dot_general | solution.py:73
  176.0 7.0 %convolution_convert_fusion.3 = bf16[768,2048]{1,0:T(8,128)(2,1)} fusion(bf16[1024,768]{0,1:T(8,128)(2,1)S(1)} %copy-done.4, bf16[1024,2048]{1,0:T(8,128)(2,1)} %bitcast.8), kind=kOutput, calls=%fused_computation.4 | convolution fusion | flops 3222798336 | bytes 8912896 | tf_op jit(solution)/shard_map/dot_general | solution.py:52
  183.0 10.3 %add_convert_fusion = bf16[1024,2048]{1,0:T(8,128)(2,1)} fusion(f32[1024,2048]{1,0:T(8,128)} %fusion, bf16[1024,768]{0,1:T(8,128)(2,1)} %get-tuple-element.9, bf16[1,768,2048]{2,1,0:T(8,128)(2,1)} %param.12), kind=kOutput, calls=%fused_computation | convolution fusion | flops 3225419776 | bytes 17301504 | tf_op jit(solution)/shard_map/dot_general | solution.py:74
  193.3 7.4 %all-to-all-start.2 = ((bf16[32,32,2048]{2,1,0:T(8,128)(2,1)}), bf16[32,32,2048]{2,1,0:T(8,128)(2,1)}, u32[]{:S(2)}, u32[]{:S(2)}) async-start(bf16[32,32,2048]{2,1,0:T(8,128)(2,1)} %bitcast.50), calls=%async_computation.2 | async-start | bytes 8388608 | tf_op jit(solution)/shard_map/all_to_all | solution.py:19
  200.7 0.5 broadcast.25
  201.2 0.7 reduce.3
  202.0 0.3 select_reduce_fusion.1
  202.3 0.6 maximum_divide_fusion
  202.9 48.6 %all-to-all-done.2 = bf16[32,32,2048]{2,1,0:T(8,128)(2,1)} async-done(((bf16[32,32,2048]{2,1,0:T(8,128)(2,1)}), bf16[32,32,2048]{2,1,0:T(8,128)(2,1)}, u32[]{:S(2)}, u32[]{:S(2)}) %all-to-all-start.2) | async-done | bytes 4194336 | tf_op jit(solution)/shard_map/all_to_all | solution.py:19
  251.6 4.5 %convolution_convert_fusion.5 = bf16[256,2048]{1,0:T(8,128)(2,1)} fusion(bf16[1024,2048]{1,0:T(8,128)(2,1)} %bitcast.12, s32[256]{0:T(256)S(1)} %fusion.18, s32[256]{0:T(256)S(1)} %fusion.17), kind=kOutput, calls=%fused_computation.19 | convolution fusion | flops 1075576832 | bytes 5244928 | tf_op jit(solution)/shard_map/dot_general | solution.py:52
  256.1 2.5 bitcast_convert_fusion
  258.6 2.5 bitcast_convert_fusion.2
  261.0 2.0 reduce-scatter.6.cloned.1.call-done
  263.0 2.5 bitcast_convert_fusion.1
  (21 shorter events, 0.6 us)
Async XLA Ops:
  7.2 73.2 %copy-start = (bf16[1,768,2048]{2,1,0:T(8,128)(2,1)S(1)}, bf16[1,768,2048]{2,1,0:T(8,128)(2,1)}, u32[]{:S(2)}) copy-start(bf16[1,768,2048]{2,1,0:T(8,128)(2,1)} %param.11) | copy-start | bytes 9437188
  12.9 7.8 %copy-start.1 = (bf16[256,2]{0,1:T(2,128)(2,1)S(1)}, bf16[256,2]{0,1:T(2,128)(2,1)}, u32[]{:S(2)}) copy-start(bf16[256,2]{0,1:T(2,128)(2,1)} %param.10) | copy-start | bytes 3076
  12.9 58.6 %all-to-all-start.1 = ((bf16[32,32,2048]{2,1,0:T(8,128)(2,1)}), bf16[32,32,2048]{2,1,0:T(8,128)(2,1)}, u32[]{:S(2)}, u32[]{:S(2)}) async-start(bf16[32,32,2048]{2,1,0:T(8,128)(2,1)} %bitcast.49), calls=%async_computation.1 | async-start | bytes 8388608 | tf_op jit(solution)/shard_map/all_to_all | solution.py:19
  71.6 59.4 %all-to-all-start = ((bf16[32,32,2048]{2,1,0:T(8,128)(2,1)}), bf16[32,32,2048]{2,1,0:T(8,128)(2,1)}, u32[]{:S(2)}, u32[]{:S(2)}) async-start(bf16[32,32,2048]{2,1,0:T(8,128)(2,1)} %bitcast.51), calls=%async_computation | async-start | bytes 8388608 | tf_op jit(solution)/shard_map/all_to_all | solution.py:19
  80.1 176.0 %reduce-scatter.8.cloned.1.call-start = ((), (), s32[]{:S(2)}) async-start(), calls=%async_computation.9 | async-start | bytes 3932160 | tf_op jit(solution)/shard_map/reduce_scatter | solution.py:65
  80.4 7.5 %copy-start.2 = (bf16[1,768,2048]{2,1,0:T(8,128)(2,1)S(1)}, bf16[1,768,2048]{2,1,0:T(8,128)(2,1)}, u32[]{:S(2)}) copy-start(bf16[1,768,2048]{2,1,0:T(8,128)(2,1)} %param.12) | copy-start | bytes 9437188
  140.2 118.4 %reduce-scatter.4.cloned.1.call-start = ((), (), s32[]{:S(2)}) async-start(), calls=%async_computation.7 | async-start | bytes 3932160 | tf_op jit(solution)/shard_map/reduce_scatter | solution.py:65
  151.1 1.1 copy-start.3
  160.2 33.1 %all-to-all-start.3 = ((f32[32,1,32]{2,1,0:T(1,128)}), f32[32,1,32]{2,1,0:T(1,128)S(1)}, u32[]{:S(2)}, u32[]{:S(2)}) async-start(f32[32,1,32]{2,1,0:T(1,128)} %all_to_all.18), calls=%async_computation.3 | async-start | bytes 32768 | tf_op jit(solution)/shard_map/all_to_all | solution.py:19
  168.5 94.6 %reduce-scatter.6.cloned.1.call-start = ((), (), s32[]{:S(2)}) async-start(), calls=%async_computation.8 | async-start | bytes 3932160 | tf_op jit(solution)/shard_map/reduce_scatter | solution.py:65
  168.8 7.2 %copy-start.4 = (bf16[1024,768]{0,1:T(8,128)(2,1)S(1)}, bf16[1024,768]{0,1:T(8,128)(2,1)}, u32[]{:S(2)}) copy-start(bf16[1024,768]{0,1:T(8,128)(2,1)} %get-tuple-element.9) | copy-start | bytes 4718596
  193.3 58.3 %all-to-all-start.2 = ((bf16[32,32,2048]{2,1,0:T(8,128)(2,1)}), bf16[32,32,2048]{2,1,0:T(8,128)(2,1)}, u32[]{:S(2)}, u32[]{:S(2)}) async-start(bf16[32,32,2048]{2,1,0:T(8,128)(2,1)} %bitcast.50), calls=%async_computation.2 | async-start | bytes 8388608 | tf_op jit(solution)/shard_map/all_to_all | solution.py:19
Sparse Core Ops, SparseCore 0:
  140.3 41.6 reduce-scatter.7
  184.4 38.0 reduce-scatter.3
  224.9 38.0 reduce-scatter.5

commit v2 on v1

v2 whole, which is shorter than its diff:
```python
import functools

import jax
import jax.numpy as jnp
from jax import lax
from jax.experimental import pallas as pl
from jax.experimental.pallas import tpu as pltpu
from jax.sharding import PartitionSpec as P

F32 = jnp.float32
BF16 = jnp.bfloat16
MESH = pl.DeviceIdType.MESH
NT = (((1,), (1,)), ((), ()))
TN = (((0,), (0,)), ((), ()))
NN = (((1,), (0,)), ((), ()))

RINGS = (
    ((2, 0), (0, 2), (2, 2)),
    ((2, 1), (1, 2), (2, 3), (3, 2)),
    ((1, 1), (3, 3), (1, 3), (3, 1)),
    ((1, 0), (0, 1), (3, 0), (0, 3)),
)
SHIFTS = [(0, 0, 0), (0, 0, 1)] + [
    (dx, dy, dc) for ring in RINGS for dc in (0, 1) for dx, dy in ring
]
CAP = 32
GROUP = 8
ROWS = GROUP * CAP
HALVES = 8
PIECES = 4


def dot(a, b, dims):
    return lax.dot_general(a, b, dims, preferred_element_type=F32)


def kernel(
    tok_ref,
    dy_ref,
    routes_ref,
    probs_ref,
    wg_hbm,
    wu_hbm,
    wd_hbm,
    dtok_ref,
    dprob_ref,
    gg_ref,
    gu_ref,
    gd_ref,
    pick,
    pick_scaled,
    xs,
    ss,
    xr,
    sr,
    wgu,
    wd,
    dgu,
    act,
    back_s,
    back_r,
    far_r,
    near_r,
    w_sem,
    fwd_s,
    fwd_r,
    back_ss,
    back_rs,
    sum_s,
    sum_r,
):
    me, z = lax.axis_index("expert"), lax.axis_index("dp")
    cx, cy, core = me // 8, (me // 2) % 4, me % 2
    up, down, across = (z + 1) % 4, (z + 3) % 4, (z + 2) % 4
    n_shift = len(SHIFTS)
    groups = n_shift // GROUP
    width = tok_ref.shape[1]
    half = wd.shape[1]

    def owner(i):
        dx, dy, dc = SHIFTS[i]
        return ((cx + dx) % 4) * 8 + ((cy + dy) % 4) * 2 + (core + dc) % 2

    def source(i):
        dx, dy, dc = SHIFTS[i]
        return ((cx + 4 - dx) % 4) * 8 + ((cy + 4 - dy) % 4) * 2 + (core + dc) % 2

    barrier = pltpu.get_barrier_semaphore()
    for i in range(1, n_shift):
        pl.semaphore_signal(barrier, inc=1, device_id=(owner(i), z), device_id_type=MESH)
    for other in (up, down):
        pl.semaphore_signal(barrier, inc=1, device_id=(me, other), device_id_type=MESH)

    loads = [
        pltpu.make_async_copy(wg_hbm, wgu.at[:, 0:half], w_sem.at[0]),
        pltpu.make_async_copy(wu_hbm, wgu.at[:, half : 2 * half], w_sem.at[1]),
        pltpu.make_async_copy(wd_hbm, wd, w_sem.at[2]),
    ]
    for load in loads:
        load.start()

    n_tok = tok_ref.shape[0]
    lane = lax.broadcasted_iota(jnp.int32, (n_tok, 128), 1)
    place = jnp.zeros((1, 128), jnp.int32)
    for i in range(1, n_shift):
        place = place + jnp.where(lane[0:1] == owner(i), i * CAP, 0)
    earlier = (
        lax.broadcasted_iota(jnp.int32, (n_tok, n_tok), 0)
        > lax.broadcasted_iota(jnp.int32, (n_tok, n_tok), 1)
    )
    earlier = jnp.where(earlier, 1.0, 0.0).astype(BF16)
    slot = lax.broadcasted_iota(jnp.int32, (n_tok, n_shift * CAP), 1)
    offset = place.astype(F32)
    scaled = jnp.zeros((n_tok, n_shift * CAP), F32)
    for k in range(2):
        named = lane == routes_ref[:, k : k + 1]
        hot = jnp.where(named, 1.0, 0.0)
        rank = dot(earlier, hot.astype(BF16), NN) + offset
        offset = offset + jnp.sum(hot, axis=0, keepdims=True)
        target = jnp.sum(jnp.where(named, rank, 0.0), axis=1, keepdims=True)
        chosen = slot == target.astype(jnp.int32)
        pick[k] = jnp.where(chosen, 1.0, 0.0).astype(BF16)
        scaled = scaled + jnp.where(chosen, probs_ref[:, k : k + 1].astype(F32), 0.0)
    pick_scaled[...] = scaled.astype(BF16)

    def forward_copy(i, piece, device):
        src, dst = (xs, xr) if piece < PIECES // 2 else (ss, sr)
        step = 2 * CAP // PIECES
        at = pl.ds(i * CAP + (piece % (PIECES // 2)) * step, step)
        return pltpu.make_async_remote_copy(
            src_ref=src.at[at],
            dst_ref=dst.at[at],
            send_sem=fwd_s.at[i, piece],
            recv_sem=fwd_r.at[i, piece],
            device_id=(device, z),
            device_id_type=MESH,
        )

    for g in range(groups):
        at = slice(g * ROWS, (g + 1) * ROWS)
        both = pick[0, :, at] + pick[1, :, at]
        xs[at] = dot(both, tok_ref[...], TN).astype(BF16)
        ss[at] = dot(pick_scaled[:, at], dy_ref[...], TN).astype(BF16)
        if g == 0:
            pl.semaphore_wait(barrier, n_shift + 1)
        for piece in range(PIECES):
            for i in range(max(1, g * GROUP), (g + 1) * GROUP):
                forward_copy(i, piece, owner(i)).start()
    xr[0:CAP] = xs[0:CAP]
    sr[0:CAP] = ss[0:CAP]
    for load in loads:
        load.wait()

    def back_copy(i, device):
        at = slice(i * CAP, (i + 1) * CAP)
        return pltpu.make_async_remote_copy(
            src_ref=back_s.at[at],
            dst_ref=back_r.at[at],
            send_sem=back_ss.at[i],
            recv_sem=back_rs.at[i],
            device_id=(device, z),
            device_id_type=MESH,
        )

    def row_gradients(g):
        at = pl.ds(pl.multiple_of(g * ROWS, ROWS), ROWS)
        lhs = dgu[:, :, at].reshape(HALVES * 2 * half, ROWS)

        def tile(n, _):
            cols = pl.ds(pl.multiple_of(n * 512, 512), 512)
            rhs = wgu[:, :, cols].reshape(HALVES * 2 * half, 512)
            back_s[at, cols] = dot(lhs, rhs, TN).astype(BF16)
            return 0

        lax.fori_loop(0, width // 512, tile, 0)

    def work(g, _):
        def arrived(i, _):
            for piece in range(PIECES):
                forward_copy(i, piece, me).wait_recv()
            return 0

        lax.fori_loop(jnp.maximum(g * GROUP, 1), (g + 1) * GROUP, arrived, 0)
        at = pl.ds(pl.multiple_of(g * ROWS, ROWS), ROWS)

        def tile(h, total):
            pre = dot(wgu[h], xr[at], NT)
            scaled_back = dot(wd[h], sr[at], NT)
            gate, upward = pre[0:half], pre[half : 2 * half]
            sig = jax.nn.sigmoid(gate)
            silu = gate * sig
            active = silu * upward
            act[h, :, at] = active.astype(BF16)
            d_gate = scaled_back * upward * (sig + silu * (1.0 - sig))
            dgu[h, 0:half, at] = d_gate.astype(BF16)
            dgu[h, half : 2 * half, at] = (scaled_back * silu).astype(BF16)
            return total + jnp.sum(active * scaled_back, axis=0, keepdims=True)

        total = lax.fori_loop(0, HALVES, tile, jnp.zeros((1, ROWS), F32))
        high = total.astype(BF16).astype(F32)
        line = lax.broadcasted_iota(jnp.int32, (128, ROWS), 0)
        pair = jnp.where(line == 0, high, jnp.where(line == 1, total - high, 0.0))
        back_s[at, width : width + 128] = pair.T.astype(BF16)

        @pl.when(g < groups - 1)
        def _():
            row_gradients(g)

        return 0

    lax.fori_loop(0, groups, work, 0)

    last = (groups - 1) * GROUP
    for i in range(1, last):
        back_copy(i, source(i)).start()

    def sent(i, _):
        for piece in range(PIECES):
            forward_copy(i, piece, me).wait_send()
        return 0

    lax.fori_loop(1, n_shift, sent, 0)

    def half_shard(h, finish):
        def tile(n, _):
            cols = pl.ds(pl.multiple_of(n * 512, 512), 512)
            finish(0, cols, dot(dgu[h], xr[:, cols], NN))
            finish(2 * half, cols, dot(act[h], sr[:, cols], NN))
            return 0

        lax.fori_loop(0, width // 512, tile, 0)

    block = 3 * half

    def sum_copy(i, src, dst, device):
        return pltpu.make_async_remote_copy(
            src_ref=src,
            dst_ref=dst,
            send_sem=sum_s.at[i],
            recv_sem=sum_r.at[i],
            device_id=(me, device),
            device_id_type=MESH,
        )

    def send_half(i, h, src, first, dst, device, add=None):
        def finish(row, cols, value):
            if add is not None:
                value = value + add[pl.ds(row, value.shape[0]), cols].astype(F32)
            src[pl.ds(first + row, value.shape[0]), cols] = value.astype(BF16)

        half_shard(h, finish)
        copy = sum_copy(i, src.at[pl.ds(first, block)], dst, device)
        copy.start()
        return copy

    far_up = send_half(0, 2 * across, xs, 0, far_r.at[0], up)
    far_down = send_half(1, 2 * across + 1, xs, block, far_r.at[1], down)
    near = [
        send_half(2, 2 * up + 1, xs, 2 * block, near_r.at[0, 1], up),
        send_half(3, 2 * down, ss, 0, near_r.at[1, 0], down),
    ]
    row_gradients(groups - 1)
    for i in range(last, n_shift):
        back_copy(i, source(i)).start()
    far_up.wait_recv()
    near.append(send_half(4, 2 * up, ss, block, near_r.at[0, 0], up, far_r.at[0]))
    far_down.wait_recv()
    near.append(
        send_half(5, 2 * down + 1, ss, 2 * block, near_r.at[1, 1], down, far_r.at[1])
    )

    for part in range(2):

        def keep(row, cols, value, part=part):
            low = slice(part * half, (part + 1) * half)
            if row == 0:
                gg_ref[low, cols] = value[0:half]
                gu_ref[low, cols] = value[half : 2 * half]
            else:
                gd_ref[low, cols] = value

        half_shard(2 * z + part, keep)

    back_r[0:CAP] = back_s[0:CAP]
    for i in range(1, n_shift):
        back_copy(i, me).wait_recv()

    def combine(n, _):
        cols = pl.ds(pl.multiple_of(n * 512, 512), 512)
        both = pick[0] + pick[1]
        dtok_ref[:, cols] = dot(both, back_r[:, cols], NN).astype(BF16)
        return 0

    lax.fori_loop(0, width // 512, combine, 0)
    for k in range(2):
        terms = dot(pick[k], back_r[:, width : width + 128], NN)
        dprob_ref[:, k : k + 1] = jnp.sum(terms, axis=1, keepdims=True) / probs_ref[
            :, k : k + 1
        ].astype(F32)

    for copy, part in ((near[0], 1), (near[1], 0), (near[2], 0), (near[3], 1)):
        copy.wait_recv()
    for part in range(2):
        low = slice(part * half, (part + 1) * half)
        for j, out in enumerate((gg_ref, gu_ref, gd_ref)):
            rows = slice(j * half, (j + 1) * half)
            out[low] = (
                out[low]
                + near_r[0, part, rows].astype(F32)
                + near_r[1, part, rows].astype(F32)
            )
    for copy in [far_up, far_down] + near:
        copy.wait_send()
    for i in range(1, n_shift):
        back_copy(i, me).wait_send()


def per_device(tokens, grad_out, routes, gate_probs, w_gate, w_up, w_down):
    n_tok, width = tokens.shape
    hidden = w_gate.shape[1]
    half = hidden // HALVES
    slots = len(SHIFTS) * CAP
    vmem = pl.BlockSpec(memory_space=pltpu.VMEM)
    hbm = pl.BlockSpec(memory_space=pl.ANY)
    weights = [w.reshape(HALVES, half, width) for w in (w_gate, w_up, w_down)]
    shard = jax.ShapeDtypeStruct((hidden // 4, width), F32)
    dma = pltpu.SemaphoreType.DMA
    d_tokens, d_probs, grad_g, grad_u, grad_d = pl.pallas_call(
        kernel,
        out_shape=(
            jax.ShapeDtypeStruct((n_tok, width), BF16),
            jax.ShapeDtypeStruct((n_tok, 2), F32),
            shard,
            shard,
            shard,
        ),
        in_specs=[vmem] * 4 + [hbm] * 3,
        out_specs=[vmem] * 5,
        scratch_shapes=[
            pltpu.VMEM((2, n_tok, slots), BF16),
            pltpu.VMEM((n_tok, slots), BF16),
            pltpu.VMEM((slots, width), BF16),
            pltpu.VMEM((slots, width), BF16),
            pltpu.VMEM((slots, width), BF16),
            pltpu.VMEM((slots, width), BF16),
            pltpu.VMEM((HALVES, 2 * half, width), BF16),
            pltpu.VMEM((HALVES, half, width), BF16),
            pltpu.VMEM((HALVES, 2 * half, slots), BF16),
            pltpu.VMEM((HALVES, half, slots), BF16),
            pltpu.VMEM((slots, width + 128), BF16),
            pltpu.VMEM((slots, width + 128), BF16),
            pltpu.VMEM((2, 3 * half, width), BF16),
            pltpu.VMEM((2, 2, 3 * half, width), BF16),
            dma((3,)),
            dma((len(SHIFTS), PIECES)),
            dma((len(SHIFTS), PIECES)),
            dma((len(SHIFTS),)),
            dma((len(SHIFTS),)),
            dma((6,)),
            dma((6,)),
        ],
        compiler_params=pltpu.CompilerParams(
            collective_id=0, has_side_effects=True, vmem_limit_bytes=62 << 20
        ),
        name="routed_backward",
    )(tokens, grad_out, routes, gate_probs, *weights)
    return d_tokens, d_probs, grad_g[None], grad_u[None], grad_d[None]


def solution(mesh):
    rows, experts = P(("expert", "dp"), None), P("expert", None, None)
    split = P("expert", "dp", None)
    return jax.shard_map(
        per_device,
        mesh=mesh,
        in_specs=(rows, rows, rows, rows, experts, experts, experts),
        out_specs=(rows, rows, split, split, split),
        check_vma=False,
    )
```

time: 274 us -> 211 us (0.77)
  Pallas kernels: 0 us -> 196 us
  waiting for transfers between devices: 133 us -> 0 us
  matrix products: 80.1 us -> 0 us
  starting transfers between devices: 32.8 us -> 0 us
  between operations: 13.9 us -> 0.65 us
  other arithmetic: 9.15 us -> 0 us
  local copies, waits for them, and re-layouts: 3.3 us -> 12 us
    pallas_call x0 -> x1, Pallas kernels: none -> 196 us  [per_device(): pl.pallas_call(kernel, out_shape=(jax.ShapeDtypeStruct((n_tok, width), BF...]
    all_to_all x4 -> x0, waiting for transfers between devices: 131 us -> none  [swap(): return lax.all_to_all(a, 'expert', split_axis=0, concat_axis=0, tiled=True)]
    dot_general x13 -> x0, matrix products: 80.1 us -> none  [the longest x7 53.4 us: dot(): return lax.dot_general(a, b, dims, preferred_element_type=F32)]
    all_to_all x4 -> x0, starting transfers between devices: 32 us -> none  [swap(): return lax.all_to_all(a, 'expert', split_axis=0, concat_axis=0, tiled=True)]
    unnamed x10 -> x13, local copies, waits for them, and re-layouts: 1.17 us -> 12 us
    broadcast_in_dim x3 -> x0, other arithmetic: 7.41 us -> none  [reduce_rows(): lax.psum_scatter(a.astype(BF16), 'dp', scatter_dimension=0, tiled=True)]
  transfers between devices with their start and end apart: 7 -> 0, of which waited for: 4 -> 0; matrix products, arithmetic and copies ran while one was open for 27% -> 0% of each run, Pallas kernels for 0% -> 0%
where the time goes in v2:
time: 211 us; the launch traced here: 209 us
  Pallas kernels  196 us (93%)
  local copies, waits for them, and re-layouts  12 us (6%)
    pallas_call x1, Pallas kernels, per_device(): pl.pallas_call(kernel, out_shape=(jax.ShapeDtypeStruct((n_tok, width), BF...  196 us
    unnamed x13, local copies, waits for them, and re-layouts  12 us

profile of v2, /device:TPU:4, one launch (start us, length us, event | category | flops | bytes accessed | tf_op | source)
XLA Modules:
  0.0 208.9 jit_solution(7450554156539637155)
XLA Ops:
  0.6 1.4 copy.13.probs_ref
  2.1 1.5 copy.12.routes_ref
  3.5 196.2 %routed_backward.1 = (bf16[256,2048]{1,0:T(8,128)(2,1)}, f32[256,2]{1,0:T(8,128)}, f32[192,2048]{1,0:T(8,128)}, f32[192,2048]{1,0:T(8,128)}, f32[192,2048]{1,0:T(8,128)}) custom-call(bf16[256,2048]{1,0:T(8,128)(2,1)} %tok_ref.1, bf16[256,2048]{1,0:T(8,128)(2,1)} %dy_ref.1, s32[256,2]{1,0:T(8,128)} %copy.12.routes_ref, bf16[256,2]{1,0:T(8,128)(2,1)} %copy.13.probs_ref, ...), custom_call_target="tpu_custom_call" | custom-call | tf_op jit(solution)/shard_map/routed_backward/pallas_call | solution.py:328
  199.8 0.0 copy-start.2
  199.8 1.7 copy.14
  201.5 2.3 %copy.19 = bf16[256,2048]{1,0:T(8,128)(2,1)} copy(bf16[256,2048]{1,0:T(8,128)(2,1)} %get-tuple-element.25) | data formatting | bytes 2097152
  203.8 0.0 copy-done.2
  203.8 0.0 copy-start.1
  203.8 1.1 copy.20
  204.9 0.8 copy-done.1
  205.7 0.0 copy-start
  205.7 1.1 copy.21
  206.9 0.8 copy-done
  207.7 1.1 copy.22
Async XLA Ops:
  199.8 4.0 %copy-start.2 = (f32[192,2048]{1,0:T(8,128)S(1)}, f32[192,2048]{1,0:T(8,128)}, u32[]{:S(2)}) copy-start(f32[192,2048]{1,0:T(8,128)} %get-tuple-element.12) | copy-start | bytes 4718596
  203.8 2.0 copy-start.1
  205.7 2.0 copy-start

commit v3 on v1

v3 whole, which is shorter than its diff:
```python
import functools

import jax
import jax.numpy as jnp
from jax import lax
from jax.experimental import pallas as pl
from jax.experimental.pallas import tpu as pltpu
from jax.sharding import PartitionSpec as P

F32 = jnp.float32
BF16 = jnp.bfloat16
MESH = pl.DeviceIdType.MESH
NT = (((1,), (1,)), ((), ()))
TN = (((0,), (0,)), ((), ()))
NN = (((1,), (0,)), ((), ()))

RINGS = (
    ((2, 0), (0, 2), (2, 2)),
    ((2, 1), (1, 2), (2, 3), (3, 2)),
    ((1, 1), (3, 3), (1, 3), (3, 1)),
    ((1, 0), (0, 1), (3, 0), (0, 3)),
)
SHIFTS = [(0, 0, 0), (0, 0, 1)] + [
    (dx, dy, dc) for ring in RINGS for dc in (0, 1) for dx, dy in ring
]
CAP = 32
GROUP = 8
ROWS = GROUP * CAP
COLS = 512
HALVES = 8


def dot(a, b, dims):
    return lax.dot_general(a, b, dims, preferred_element_type=F32)


def kernel(
    tok_ref,
    dy_ref,
    routes_ref,
    probs_ref,
    wg_hbm,
    wu_hbm,
    wd_hbm,
    dtok_ref,
    dprob_ref,
    own_gu_hbm,
    own_d_hbm,
    near_gu,
    near_d,
    pick,
    pick_scaled,
    xs,
    ss,
    xr,
    sr,
    wgu,
    wd,
    dgu,
    act,
    slope,
    silus,
    backs,
    own_d,
    back_s,
    back_r,
    far_gu,
    far_d,
    w_sem,
    x_s,
    x_r,
    s_s,
    s_r,
    back_ss,
    back_rs,
    gu_s,
    gu_r,
    d_s,
    d_r,
    own_sem,
):
    me, z = lax.axis_index("expert"), lax.axis_index("dp")
    cx, cy, core = me // 8, (me // 2) % 4, me % 2
    up, down, across = (z + 1) % 4, (z + 3) % 4, (z + 2) % 4
    n_shift = len(SHIFTS)
    groups = n_shift // GROUP
    n_tok, width = tok_ref.shape
    chunks = width // COLS
    half = wd.shape[0] // HALVES

    def owner(i):
        dx, dy, dc = SHIFTS[i]
        return ((cx + dx) % 4) * 8 + ((cy + dy) % 4) * 2 + (core + dc) % 2

    def source(i):
        dx, dy, dc = SHIFTS[i]
        return ((cx + 4 - dx) % 4) * 8 + ((cy + 4 - dy) % 4) * 2 + (core + dc) % 2

    def remote(src, dst, send_sem, recv_sem, device):
        return pltpu.make_async_remote_copy(
            src_ref=src,
            dst_ref=dst,
            send_sem=send_sem,
            recv_sem=recv_sem,
            device_id=device,
            device_id_type=MESH,
        )

    barrier = pltpu.get_barrier_semaphore()
    for i in range(1, n_shift):
        pl.semaphore_signal(barrier, inc=1, device_id=(owner(i), z), device_id_type=MESH)
    for other in (up, down):
        pl.semaphore_signal(barrier, inc=1, device_id=(me, other), device_id_type=MESH)

    loads = [
        pltpu.make_async_copy(wd_hbm, wd, w_sem.at[0]),
    ]
    for h in range(HALVES):
        for j, w in enumerate((wg_hbm, wu_hbm)):
            loads.append(
                pltpu.make_async_copy(
                    w.at[h * half : (h + 1) * half],
                    wgu.at[(2 * h + j) * half : (2 * h + j + 1) * half],
                    w_sem.at[1 + 2 * h + j],
                )
            )
    for load in loads:
        load.start()

    line = lax.broadcasted_iota(jnp.int32, (128, n_tok), 0)
    routes = routes_ref[...].astype(F32)
    probs = probs_ref[...].astype(F32)
    table = jnp.where(line == 0, routes[0:1], routes[1:2])
    table = jnp.where(line == 2, probs[0:1], table)
    table = jnp.where(line == 3, probs[1:2], table).T
    lane = lax.broadcasted_iota(jnp.int32, (n_tok, 128), 1)
    place = jnp.zeros((1, 128), jnp.int32)
    for i in range(1, n_shift):
        place = place + jnp.where(lane[0:1] == owner(i), i * CAP, 0)
    earlier = (
        lax.broadcasted_iota(jnp.int32, (n_tok, n_tok), 0)
        > lax.broadcasted_iota(jnp.int32, (n_tok, n_tok), 1)
    )
    earlier = jnp.where(earlier, 1.0, 0.0).astype(BF16)
    slot = lax.broadcasted_iota(jnp.int32, (n_tok, n_shift * CAP), 1)
    offset = place.astype(F32)
    scaled = jnp.zeros((n_tok, n_shift * CAP), F32)
    for k in range(2):
        named = lane == table[:, k : k + 1].astype(jnp.int32)
        hot = jnp.where(named, 1.0, 0.0)
        rank = dot(earlier, hot.astype(BF16), NN) + offset
        offset = offset + jnp.sum(hot, axis=0, keepdims=True)
        target = jnp.sum(jnp.where(named, rank, 0.0), axis=1, keepdims=True)
        chosen = slot == target.astype(jnp.int32)
        pick[k] = jnp.where(chosen, 1.0, 0.0).astype(BF16)
        scaled = scaled + jnp.where(chosen, table[:, 2 + k : 3 + k], 0.0)
    pick_scaled[...] = scaled.astype(BF16)

    for g in range(groups):
        at = slice(g * ROWS, (g + 1) * ROWS)
        both = pick[0, :, at] + pick[1, :, at]
        for c in range(chunks):
            cols = slice(c * COLS, (c + 1) * COLS)
            xs[c, at] = dot(both, tok_ref[:, cols], TN).astype(BF16)
        if g == 0:
            pl.semaphore_wait(barrier, n_shift + 1)
        for c in range(chunks):
            for i in range(max(1, g * GROUP), (g + 1) * GROUP):
                rows = slice(i * CAP, (i + 1) * CAP)
                remote(
                    xs.at[c, rows], xr.at[c, rows], x_s, x_r.at[g], (owner(i), z)
                ).start()
    for c in range(chunks):
        cols = slice(c * COLS, (c + 1) * COLS)
        for g in range(groups):
            at = slice(g * ROWS, (g + 1) * ROWS)
            ss[c, at] = dot(pick_scaled[:, at], dy_ref[:, cols], TN).astype(BF16)
        for i in range(1, n_shift):
            rows = slice(i * CAP, (i + 1) * CAP)
            remote(
                ss.at[c, rows], sr.at[c, rows], s_s, s_r.at[c], (owner(i), z)
            ).start()
    for c in range(chunks):
        xr[c, 0:CAP] = xs[c, 0:CAP]
        sr[c, 0:CAP] = ss[c, 0:CAP]
    for load in loads:
        load.wait()

    for g in range(groups):
        first = CAP if g == 0 else g * ROWS
        took = slice(first, (g + 1) * ROWS)
        remote(xs.at[:, took], xr.at[:, took], x_s, x_r.at[g], (me, z)).wait_recv()
        at = slice(g * ROWS, (g + 1) * ROWS)

        def project(t, _, at=at):
            rows = pl.ds(pl.multiple_of(t * 4 * half, 4 * half), 4 * half)
            pre = jnp.zeros((4 * half, ROWS), F32)
            for c in range(chunks):
                cols = slice(c * COLS, (c + 1) * COLS)
                pre = pre + dot(wgu[rows, cols], xr[c, at], NT)
            for j in range(2):
                gate = pre[2 * j * half : (2 * j + 1) * half]
                upward = pre[(2 * j + 1) * half : (2 * j + 2) * half]
                into = pl.ds(pl.multiple_of((2 * t + j) * half, half), half)
                sig = jax.nn.sigmoid(gate)
                silu = gate * sig
                act[into, at] = (silu * upward).astype(BF16)
                slope[into, at] = upward * (sig + silu * (1.0 - sig))
                silus[into, at] = silu
            return 0

        lax.fori_loop(0, HALVES // 2, project, 0)

    sent = slice(CAP, n_shift * CAP)
    remote(xs.at[:, sent], xr.at[:, sent], x_s, x_r.at[0], (me, z)).wait_send()

    def part_rows(h, size):
        return pl.ds(pl.multiple_of(h * size, size), size)

    def down_half(h, c):
        return dot(act[part_rows(h, half)], sr[c], NN)

    D_ROWS = [slice(k * half, (k + 1) * half) for k in range(6)]

    def down_copy(k, c):
        dst = (
            far_d.at[0, c],
            far_d.at[1, c],
            near_d.at[0, 1, c],
            near_d.at[1, 0, c],
            near_d.at[0, 0, c],
            near_d.at[1, 1, c],
        )[k]
        return remote(
            xs.at[c, D_ROWS[k]],
            dst,
            d_s.at[k, c],
            d_r.at[k, c],
            (me, up if k % 2 == 0 else down),
        )

    halves = (2 * across, 2 * across + 1, 2 * up + 1, 2 * down, 2 * up, 2 * down + 1)

    def down_first(c):
        for k in range(4):
            xs[c, D_ROWS[k]] = down_half(halves[k], c).astype(BF16)
            down_copy(k, c).start()
        for part in range(2):
            own_d[(part * chunks + c) * half : (part * chunks + c + 1) * half] = (
                down_half(2 * z + part, c)
            )

    def down_second(c):
        for k in range(4, 6):
            value = down_half(halves[k], c)
            down_copy(k - 4, c).wait_recv()
            xs[c, D_ROWS[k]] = (value + far_d[k - 4, c].astype(F32)).astype(BF16)
            down_copy(k, c).start()

    def chunk_arrived(c):
        remote(ss.at[c, sent], sr.at[c, sent], s_s, s_r.at[c], (me, z)).wait_recv()

    big = 4 * half
    for c in range(chunks - 1):
        cols = slice(c * COLS, (c + 1) * COLS)
        chunk_arrived(c)
        down_first(c)

        def project_back(t, _, c=c, cols=cols):
            rows = part_rows(t, big)
            value = dot(wd[rows, cols], sr[c], NT)
            backs[rows] = value if c == 0 else backs[rows] + value
            return 0

        lax.fori_loop(0, HALVES // 4, project_back, 0)
        down_second(c)

    chunk_arrived(chunks - 1)
    remote(ss.at[:, sent], sr.at[:, sent], s_s, s_r.at[0], (me, z)).wait_send()
    last_cols = slice((chunks - 1) * COLS, chunks * COLS)

    def finish_half(h):
        rows = part_rows(h, half)
        back = backs[rows] + dot(wd[rows, last_cols], sr[chunks - 1], NT)
        dgu[pl.ds(pl.multiple_of(2 * h * half, 2 * half), half)] = (
            back * slope[rows]
        ).astype(BF16)
        dgu[pl.ds(pl.multiple_of((2 * h + 1) * half, half), half)] = (
            back * silus[rows]
        ).astype(BF16)
        return jnp.sum(act[rows].astype(F32) * back, axis=0, keepdims=True)

    def gate_up_half(h, c):
        return dot(dgu[part_rows(h, 2 * half)], xr[c], NN)

    def gate_up_copy(k, c):
        dst = (
            far_gu.at[0, c],
            far_gu.at[1, c],
            near_gu.at[0, 1, c],
            near_gu.at[1, 0, c],
            near_gu.at[0, 0, c],
            near_gu.at[1, 1, c],
        )[k]
        size = 2 * half
        if k < 5:
            src = ss.at[c, k * size : (k + 1) * size]
        else:
            src = xs.at[c, 6 * half : 6 * half + size]
        return src, remote(
            src,
            dst,
            gu_s.at[k, c],
            gu_r.at[k, c],
            (me, up if k % 2 == 0 else down),
        )

    def send_gate_up(k):
        def tile(c, _):
            value = gate_up_half(halves[k], c)
            src, copy = gate_up_copy(k, c)
            if k >= 4:
                gate_up_copy(k - 4, c)[1].wait_recv()
                value = value + far_gu[k - 4, c].astype(F32)
            src[...] = value.astype(BF16)
            copy.start()
            return 0

        lax.fori_loop(0, chunks, tile, 0)

    total = finish_half(halves[0])
    send_gate_up(0)
    total = total + finish_half(halves[1])
    send_gate_up(1)
    total = lax.fori_loop(
        2, HALVES, lambda i, t: t + finish_half((2 * across + i) % HALVES), total
    )
    high = total.astype(BF16).astype(F32)
    for g in range(groups):
        at = slice(g * ROWS, (g + 1) * ROWS)
        line = lax.broadcasted_iota(jnp.int32, (128, ROWS), 0)
        pair = jnp.where(line == 0, high[:, at], 0.0)
        pair = jnp.where(line == 1, (total - high)[:, at], pair)
        back_s[at, width : width + 128] = pair.T.astype(BF16)

    def back_copy(i, piece, device):
        at = slice(i * CAP + piece * CAP // 2, i * CAP + (piece + 1) * CAP // 2)
        return remote(back_s.at[at], back_r.at[at], back_ss, back_rs, (device, z))

    def return_rows(g):
        at = slice(g * ROWS, (g + 1) * ROWS)

        def tile(n, _):
            cols = pl.ds(pl.multiple_of(n * COLS, COLS), COLS)
            back_s[at, cols] = dot(dgu[:, at], wgu[:, cols], TN).astype(BF16)
            return 0

        lax.fori_loop(0, chunks, tile, 0)
        for piece in range(2):
            for i in range(max(1, g * GROUP), (g + 1) * GROUP):
                back_copy(i, piece, source(i)).start()

    return_rows(0)
    send_gate_up(2)
    send_gate_up(3)
    for g in range(1, groups):
        return_rows(g)
    down_first(chunks - 1)
    send_gate_up(4)
    send_gate_up(5)
    down_second(chunks - 1)
    for part in range(2):

        def keep(c, _, part=part):
            value = gate_up_half(2 * z + part, c)
            rows = part_rows(part * chunks + c, half)
            slope[rows, 0:COLS] = value[0:half]
            slope[rows, COLS : 2 * COLS] = value[half : 2 * half]
            return 0

        lax.fori_loop(0, chunks, keep, 0)
    own = [
        pltpu.make_async_copy(slope, own_gu_hbm, own_sem.at[0]),
        pltpu.make_async_copy(own_d, own_d_hbm, own_sem.at[1]),
    ]
    for copy in own:
        copy.start()

    back_r[0:CAP] = back_s[0:CAP]
    remote(back_s.at[sent], back_r.at[sent], back_ss, back_rs, (me, z)).wait_recv()

    def combine(n, _):
        cols = pl.ds(pl.multiple_of(n * COLS, COLS), COLS)
        both = pick[0] + pick[1]
        dtok_ref[:, cols] = dot(both, back_r[:, cols], NN).astype(BF16)
        return 0

    lax.fori_loop(0, chunks, combine, 0)
    for k in range(2):
        terms = dot(pick[k], back_r[:, width : width + 128], NN).T
        dprob_ref[k : k + 1] = (
            jnp.sum(terms, axis=0, keepdims=True) / probs_ref[...].astype(F32)[k : k + 1]
        )

    def finish(c, _):
        for k in range(6):
            if k >= 2:
                down_copy(k, c).wait_recv()
                gate_up_copy(k, c)[1].wait_recv()
            down_copy(k, c).wait_send()
            gate_up_copy(k, c)[1].wait_send()
        return 0

    lax.fori_loop(0, chunks, finish, 0)
    for copy in own:
        copy.wait()
    remote(back_s.at[sent], back_r.at[sent], back_ss, back_rs, (me, z)).wait_send()


def add_up(own_gu, own_d, near_gu, near_d, tok_in, prob_in, tok, prob, gg, gu, gd):
    half = gg.shape[0]
    total = near_gu[0, 0, 0].astype(F32) + near_gu[1, 0, 0].astype(F32)
    gg[...] = own_gu[:, 0:COLS] + total[0:half]
    gu[...] = own_gu[:, COLS : 2 * COLS] + total[half : 2 * half]
    gd[...] = (
        own_d[...] + near_d[0, 0, 0].astype(F32) + near_d[1, 0, 0].astype(F32)
    )
    tok[...] = tok_in[...]
    prob[...] = prob_in[...]


def per_device(tokens, grad_out, routes, gate_probs, w_gate, w_up, w_down):
    n_tok, width = tokens.shape
    hidden = w_gate.shape[1]
    half = hidden // HALVES
    slots = len(SHIFTS) * CAP
    chunks = width // COLS
    vmem = pl.BlockSpec(memory_space=pltpu.VMEM)
    hbm = pl.BlockSpec(memory_space=pl.ANY)
    weights = [w[0] for w in (w_gate, w_up, w_down)]
    dma = pltpu.SemaphoreType.DMA
    d_tokens, d_probs, own_gu, own_d, near_gu, near_d = pl.pallas_call(
        kernel,
        out_shape=(
            jax.ShapeDtypeStruct((n_tok, width), BF16),
            jax.ShapeDtypeStruct((2, n_tok), F32),
            jax.ShapeDtypeStruct((hidden, 2 * COLS), F32),
            jax.ShapeDtypeStruct((hidden, COLS), F32),
            jax.ShapeDtypeStruct((2, 2, chunks, 2 * half, COLS), BF16),
            jax.ShapeDtypeStruct((2, 2, chunks, half, COLS), BF16),
        ),
        in_specs=[vmem] * 4 + [hbm] * 3,
        out_specs=[vmem] * 2 + [hbm] * 4,
        scratch_shapes=[
            pltpu.VMEM((2, n_tok, slots), BF16),
            pltpu.VMEM((n_tok, slots), BF16),
            pltpu.VMEM((chunks, slots, COLS), BF16),
            pltpu.VMEM((chunks, slots, COLS), BF16),
            pltpu.VMEM((chunks, slots, COLS), BF16),
            pltpu.VMEM((chunks, slots, COLS), BF16),
            pltpu.VMEM((2 * hidden, width), BF16),
            pltpu.VMEM((hidden, width), BF16),
            pltpu.VMEM((2 * hidden, slots), BF16),
            pltpu.VMEM((hidden, slots), BF16),
            pltpu.VMEM((hidden, slots), F32),
            pltpu.VMEM((hidden, slots), F32),
            pltpu.VMEM((hidden, slots), F32),
            pltpu.VMEM((hidden, COLS), F32),
            pltpu.VMEM((slots, width + 128), BF16),
            pltpu.VMEM((slots, width + 128), BF16),
            pltpu.VMEM((2, chunks, 2 * half, COLS), BF16),
            pltpu.VMEM((2, chunks, half, COLS), BF16),
            dma((1 + 2 * HALVES,)),
            dma,
            dma((len(SHIFTS) // GROUP,)),
            dma,
            dma((chunks,)),
            dma,
            dma,
            dma((6, chunks)),
            dma((6, chunks)),
            dma((6, chunks)),
            dma((6, chunks)),
            dma((2,)),
        ],
        compiler_params=pltpu.CompilerParams(
            collective_id=0, has_side_effects=True, vmem_limit_bytes=63 << 20
        ),
        name="routed_backward",
    )(tokens, grad_out, routes.T, gate_probs.T, *weights)
    step = lambda p, c: (p * chunks + c, 0)
    fixed = lambda p, c: (0, 0)
    tile = pl.BlockSpec((half, COLS), lambda p, c: (p, c))
    rows = pl.BlockSpec((n_tok // HALVES, width), step)
    row_probs = pl.BlockSpec((2, n_tok), fixed)
    shard = jax.ShapeDtypeStruct((hidden // 4, width), F32)
    d_tokens, d_probs, grad_g, grad_u, grad_d = pl.pallas_call(
        add_up,
        grid=(2, chunks),
        out_shape=(
            jax.ShapeDtypeStruct((n_tok, width), BF16),
            jax.ShapeDtypeStruct((2, n_tok), F32),
            shard,
            shard,
            shard,
        ),
        in_specs=[
            pl.BlockSpec((half, 2 * COLS), step),
            pl.BlockSpec((half, COLS), step),
            pl.BlockSpec((2, 1, 1, 2 * half, COLS), lambda p, c: (0, p, c, 0, 0)),
            pl.BlockSpec((2, 1, 1, half, COLS), lambda p, c: (0, p, c, 0, 0)),
            rows,
            row_probs,
        ],
        out_specs=[rows, row_probs, tile, tile, tile],
        name="add_up",
    )(own_gu, own_d, near_gu, near_d, d_tokens, d_probs)
    return d_tokens, d_probs.T, grad_g[None], grad_u[None], grad_d[None]


def solution(mesh):
    rows, experts = P(("expert", "dp"), None), P("expert", None, None)
    split = P("expert", "dp", None)
    return jax.shard_map(
        per_device,
        mesh=mesh,
        in_specs=(rows, rows, rows, rows, experts, experts, experts),
        out_specs=(rows, rows, split, split, split),
        check_vma=False,
    )
```

time: 274 us -> 178 us (0.65)
  Pallas kernels: 0 us -> 177 us
  waiting for transfers between devices: 133 us -> 0 us
  matrix products: 80.1 us -> 0 us
  starting transfers between devices: 32.8 us -> 0 us
  between operations: 13.9 us -> 0.74 us
  other arithmetic: 9.15 us -> 0 us
  local copies, waits for them, and re-layouts: 3.3 us -> 0 us
    pallas_call x0 -> x2, Pallas kernels: none -> 177 us  [the longest x1 168 us: per_device(): pl.pallas_call(kernel, out_shape=(jax.ShapeDtypeStruct((n_tok, width), BF...]
    all_to_all x4 -> x0, waiting for transfers between devices: 131 us -> none  [swap(): return lax.all_to_all(a, 'expert', split_axis=0, concat_axis=0, tiled=True)]
    dot_general x13 -> x0, matrix products: 80.1 us -> none  [the longest x7 53.4 us: dot(): return lax.dot_general(a, b, dims, preferred_element_type=F32)]
    all_to_all x4 -> x0, starting transfers between devices: 32 us -> none  [swap(): return lax.all_to_all(a, 'expert', split_axis=0, concat_axis=0, tiled=True)]
    broadcast_in_dim x3 -> x0, other arithmetic: 7.41 us -> none  [reduce_rows(): lax.psum_scatter(a.astype(BF16), 'dp', scatter_dimension=0, tiled=True)]
  transfers between devices with their start and end apart: 7 -> 0, of which waited for: 4 -> 0; matrix products, arithmetic and copies ran while one was open for 27% -> 0% of each run, Pallas kernels for 0% -> 0%
where the time goes in v3:
time: 178 us
  Pallas kernels  177 us (99%)
    pallas_call x1, Pallas kernels, per_device(): pl.pallas_call(kernel, out_shape=(jax.ShapeDtypeStruct((n_tok, width), BF...  168 us
    pallas_call x1, Pallas kernels, per_device(): pl.pallas_call(add_up, grid=(2, chunks), out_shape=(jax.ShapeDtypeStruct(...  8.4 us

profile of v3, /device:TPU:4, one launch (start us, length us, event | category | flops | bytes accessed | tf_op | source)
XLA Modules:
  0.0 177.6 jit_solution(11937141837732497126)
XLA Ops:
  0.6 168.5 %routed_backward.1 = (bf16[256,2048]{1,0:T(8,128)(2,1)}, f32[2,256]{1,0:T(2,128)}, f32[768,1024]{1,0:T(8,128)}, f32[768,512]{1,0:T(8,128)}, bf16[2,2,4,192,512]{...) custom-call(bf16[256,2048]{1,0:T(8,128)(2,1)} %tok_ref.1, bf16[256,2048]{1,0:T(8,128)(2,1)} %dy_ref.1, ...), custom_call_target="tpu_custom_call" | custom-call | tf_op jit(solution)/shard_map/routed_backward/pallas_call | solution.py:442
  169.1 8.4 %add_up.1 = (bf16[256,2048]{1,0:T(8,128)(2,1)}, f32[2,256]{1,0:T(2,128)}, f32[192,2048]{1,0:T(8,128)}, f32[192,2048]{1,0:T(8,128)}, f32[192,2048]{1,0:T(8,128)}) custom-call(f32[768,1024]{1,0:T(8,128)} %get-tuple-element.16.own_gu, f32[768,512]{1,0:T(8,128)} %get-tuple-element.17.own_d, bf16[2,2,4,192,512]{4,3,2,1,0:T(8,128)(2,1)} %get-tuple-element.18.near_gu, ...), custom_call_target="tpu_custom_call" | custom-call | tf_op jit(solution)/shard_map/add_up/pallas_call | solution.py:497

commit v4 on v3

--- a/solution.py
+++ b/solution.py
@@ -27,6 +27,7 @@
 GROUP = 8
 ROWS = GROUP * CAP
 COLS = 512
+PIECES = ((0, 0, 512), (1, 0, 512), (2, 0, 512), (3, 0, 256), (3, 256, 256))
 HALVES = 8
 
 
@@ -64,8 +65,12 @@
     own_d,
     back_s,
     back_r,
+    prob_s,
+    prob_r,
     far_gu,
     far_d,
+    mid_gu,
+    mid_d,
     w_sem,
     x_s,
     x_r,
@@ -73,6 +78,8 @@
     s_r,
     back_ss,
     back_rs,
+    prob_ss,
+    prob_rs,
     gu_s,
     gu_r,
     d_s,
@@ -175,11 +182,10 @@
         for g in range(groups):
             at = slice(g * ROWS, (g + 1) * ROWS)
             ss[c, at] = dot(pick_scaled[:, at], dy_ref[:, cols], TN).astype(BF16)
-        for i in range(1, n_shift):
-            rows = slice(i * CAP, (i + 1) * CAP)
-            remote(
-                ss.at[c, rows], sr.at[c, rows], s_s, s_r.at[c], (owner(i), z)
-            ).start()
+        for j, (block, low, size) in enumerate(PIECES):
+            for i in range(1, n_shift) if block == c else ():
+                at = (c, slice(i * CAP, (i + 1) * CAP), slice(low, low + size))
+                remote(ss.at[at], sr.at[at], s_s, s_r.at[j], (owner(i), z)).start()
     for c in range(chunks):
         xr[c, 0:CAP] = xs[c, 0:CAP]
         sr[c, 0:CAP] = ss[c, 0:CAP]
@@ -217,71 +223,80 @@
     def part_rows(h, size):
         return pl.ds(pl.multiple_of(h * size, size), size)
 
-    def down_half(h, c):
-        return dot(act[part_rows(h, half)], sr[c], NN)
+    def piece(j):
+        block, low, size = PIECES[j]
+        return block, slice(low, low + size)
+
+    def down_half(h, j):
+        block, cols = piece(j)
+        return dot(act[part_rows(h, half)], sr[block, :, cols], NN)
 
     D_ROWS = [slice(k * half, (k + 1) * half) for k in range(6)]
 
-    def down_copy(k, c):
-        dst = (
-            far_d.at[0, c],
-            far_d.at[1, c],
-            near_d.at[0, 1, c],
-            near_d.at[1, 0, c],
-            near_d.at[0, 0, c],
-            near_d.at[1, 1, c],
-        )[k]
+    def down_copy(k, j):
+        block, cols = piece(j)
+        dst = (far_d.at[0], far_d.at[1], mid_d.at[1], mid_d.at[0], near_d.at[0], near_d.at[1])
         return remote(
-            xs.at[c, D_ROWS[k]],
-            dst,
-            d_s.at[k, c],
-            d_r.at[k, c],
+            xs.at[block, D_ROWS[k], cols],
+            dst[k].at[block, :, cols],
+            d_s.at[k, j],
+            d_r.at[k, j],
             (me, up if k % 2 == 0 else down),
         )
 
     halves = (2 * across, 2 * across + 1, 2 * up + 1, 2 * down, 2 * up, 2 * down + 1)
 
-    def down_first(c):
+    def down_first(j):
+        block, cols = piece(j)
         for k in range(4):
-            xs[c, D_ROWS[k]] = down_half(halves[k], c).astype(BF16)
-            down_copy(k, c).start()
+            xs[block, D_ROWS[k], cols] = down_half(halves[k], j).astype(BF16)
+            down_copy(k, j).start()
         for part in range(2):
-            own_d[(part * chunks + c) * half : (part * chunks + c + 1) * half] = (
-                down_half(2 * z + part, c)
-            )
-
-    def down_second(c):
+            at = (part * chunks + block) * half
+            own_d[at : at + half, cols] = down_half(2 * z + part, j)
+
+    def down_second(j):
+        block, cols = piece(j)
         for k in range(4, 6):
-            value = down_half(halves[k], c)
-            down_copy(k - 4, c).wait_recv()
-            xs[c, D_ROWS[k]] = (value + far_d[k - 4, c].astype(F32)).astype(BF16)
-            down_copy(k, c).start()
-
-    def chunk_arrived(c):
-        remote(ss.at[c, sent], sr.at[c, sent], s_s, s_r.at[c], (me, z)).wait_recv()
+            value = down_half(halves[k], j)
+            down_copy(k - 4, j).wait_recv()
+            value = value + far_d[k - 4, block, :, cols].astype(F32)
+            xs[block, D_ROWS[k], cols] = value.astype(BF16)
+            down_copy(k, j).start()
+
+    def piece_arrived(j):
+        block, cols = piece(j)
+        at = (block, sent, cols)
+        remote(ss.at[at], sr.at[at], s_s, s_r.at[j], (me, z)).wait_recv()
+
+    def weight_cols(j):
+        block, low, size = PIECES[j]
+        return slice(block * COLS + low, block * COLS + low + size)
 
     big = 4 * half
-    for c in range(chunks - 1):
-        cols = slice(c * COLS, (c + 1) * COLS)
-        chunk_arrived(c)
-        down_first(c)
-
-        def project_back(t, _, c=c, cols=cols):
+    last = len(PIECES) - 1
+    for j in range(last):
+        block, cols = piece(j)
+        piece_arrived(j)
+        down_first(j)
+
+        def project_back(t, _, j=j, block=block, cols=cols):
             rows = part_rows(t, big)
-            value = dot(wd[rows, cols], sr[c], NT)
-            backs[rows] = value if c == 0 else backs[rows] + value
+            value = dot(wd[rows, weight_cols(j)], sr[block, :, cols], NT)
+            backs[rows] = value if j == 0 else backs[rows] + value
             return 0
 
         lax.fori_loop(0, HALVES // 4, project_back, 0)
-        down_second(c)
-
-    chunk_arrived(chunks - 1)
+        down_second(j)
+
+    piece_arrived(last)
     remote(ss.at[:, sent], sr.at[:, sent], s_s, s_r.at[0], (me, z)).wait_send()
-    last_cols = slice((chunks - 1) * COLS, chunks * COLS)
+    last_block, last_cols = piece(last)
 
     def finish_half(h):
         rows = part_rows(h, half)
-        back = backs[rows] + dot(wd[rows, last_cols], sr[chunks - 1], NT)
+        rest = dot(wd[rows, weight_cols(last)], sr[last_block, :, last_cols], NT)
+        back = backs[rows] + rest
         dgu[pl.ds(pl.multiple_of(2 * h * half, 2 * half), half)] = (
             back * slope[rows]
         ).astype(BF16)
@@ -294,14 +309,7 @@
         return dot(dgu[part_rows(h, 2 * half)], xr[c], NN)
 
     def gate_up_copy(k, c):
-        dst = (
-            far_gu.at[0, c],
-            far_gu.at[1, c],
-            near_gu.at[0, 1, c],
-            near_gu.at[1, 0, c],
-            near_gu.at[0, 0, c],
-            near_gu.at[1, 1, c],
-        )[k]
+        dst = (far_gu.at[0], far_gu.at[1], mid_gu.at[1], mid_gu.at[0], near_gu.at[0], near_gu.at[1])
         size = 2 * half
         if k < 5:
             src = ss.at[c, k * size : (k + 1) * size]
@@ -309,76 +317,104 @@
             src = xs.at[c, 6 * half : 6 * half + size]
         return src, remote(
             src,
-            dst,
+            dst[k].at[c],
             gu_s.at[k, c],
             gu_r.at[k, c],
             (me, up if k % 2 == 0 else down),
         )
 
-    def send_gate_up(k):
-        def tile(c, _):
-            value = gate_up_half(halves[k], c)
-            src, copy = gate_up_copy(k, c)
-            if k >= 4:
-                gate_up_copy(k - 4, c)[1].wait_recv()
-                value = value + far_gu[k - 4, c].astype(F32)
-            src[...] = value.astype(BF16)
-            copy.start()
-            return 0
-
-        lax.fori_loop(0, chunks, tile, 0)
-
-    total = finish_half(halves[0])
-    send_gate_up(0)
-    total = total + finish_half(halves[1])
-    send_gate_up(1)
+    def send_gate_up(k, c):
+        value = gate_up_half(halves[k], c)
+        src, copy = gate_up_copy(k, c)
+        if k >= 4:
+            gate_up_copy(k - 4, c)[1].wait_recv()
+            value = value + far_gu[k - 4, c].astype(F32)
+        src[...] = value.astype(BF16)
+        copy.start()
+
+    def return_tile(g, n):
+        at = slice(g * ROWS, (g + 1) * ROWS)
+        cols = pl.ds(pl.multiple_of(n * COLS, COLS), COLS)
+        back_s[n, at] = dot(dgu[:, at], wgu[:, cols], TN).astype(BF16)
+        for i in range(max(1, g * GROUP), (g + 1) * GROUP):
+            rows = slice(i * CAP, (i + 1) * CAP)
+            remote(
+                back_s.at[n, rows],
+                back_r.at[n, rows],
+                back_ss,
+                back_rs.at[n],
+                (source(i), z),
+            ).start()
+
+    total = finish_half(halves[0]) + finish_half(halves[1])
+    send_gate_up(0, 0)
+    send_gate_up(1, 0)
     total = lax.fori_loop(
         2, HALVES, lambda i, t: t + finish_half((2 * across + i) % HALVES), total
     )
+
+    def with_far(n, _):
+        return_tile(0, n)
+
+        @pl.when(n < chunks - 1)
+        def _():
+            send_gate_up(0, n + 1)
+            send_gate_up(1, n + 1)
+
+        return 0
+
+    lax.fori_loop(0, chunks, with_far, 0)
+
+    def with_near(n, _):
+        return_tile(1, n)
+        send_gate_up(2, n)
+        send_gate_up(3, n)
+        return 0
+
+    lax.fori_loop(0, chunks, with_near, 0)
+
     high = total.astype(BF16).astype(F32)
-    for g in range(groups):
-        at = slice(g * ROWS, (g + 1) * ROWS)
-        line = lax.broadcasted_iota(jnp.int32, (128, ROWS), 0)
-        pair = jnp.where(line == 0, high[:, at], 0.0)
-        pair = jnp.where(line == 1, (total - high)[:, at], pair)
-        back_s[at, width : width + 128] = pair.T.astype(BF16)
-
-    def back_copy(i, piece, device):
-        at = slice(i * CAP + piece * CAP // 2, i * CAP + (piece + 1) * CAP // 2)
-        return remote(back_s.at[at], back_r.at[at], back_ss, back_rs, (device, z))
-
-    def return_rows(g):
-        at = slice(g * ROWS, (g + 1) * ROWS)
-
-        def tile(n, _):
-            cols = pl.ds(pl.multiple_of(n * COLS, COLS), COLS)
-            back_s[at, cols] = dot(dgu[:, at], wgu[:, cols], TN).astype(BF16)
-            return 0
-
-        lax.fori_loop(0, chunks, tile, 0)
-        for piece in range(2):
-            for i in range(max(1, g * GROUP), (g + 1) * GROUP):
-                back_copy(i, piece, source(i)).start()
-
-    return_rows(0)
-    send_gate_up(2)
-    send_gate_up(3)
-    for g in range(1, groups):
-        return_rows(g)
-    down_first(chunks - 1)
-    send_gate_up(4)
-    send_gate_up(5)
-    down_second(chunks - 1)
+    line = lax.broadcasted_iota(jnp.int32, (128, n_shift * CAP), 0)
+    pair = jnp.where(line == 0, high, jnp.where(line == 1, total - high, 0.0))
+    prob_s[...] = pair.T.astype(BF16)
+    for i in range(1, n_shift):
+        rows = slice(i * CAP, (i + 1) * CAP)
+        remote(
+            prob_s.at[rows], prob_r.at[rows], prob_ss, prob_rs, (source(i), z)
+        ).start()
+    down_first(last)
+
+    def rest_back(n, _):
+        return_tile(2, n)
+        return_tile(3, n)
+        return 0
+
+    lax.fori_loop(0, chunks, rest_back, 0)
+
+    def with_far_sum(c, _):
+        send_gate_up(4, c)
+        send_gate_up(5, c)
+        return 0
+
+    lax.fori_loop(0, chunks, with_far_sum, 0)
+    down_second(last)
     for part in range(2):
 
         def keep(c, _, part=part):
             value = gate_up_half(2 * z + part, c)
+            gate_up_copy(3 - part, c)[1].wait_recv()
+            value = value + mid_gu[part, c].astype(F32)
             rows = part_rows(part * chunks + c, half)
             slope[rows, 0:COLS] = value[0:half]
             slope[rows, COLS : 2 * COLS] = value[half : 2 * half]
             return 0
 
         lax.fori_loop(0, chunks, keep, 0)
+        for j in range(last + 1):
+            down_copy(3 - part, j).wait_recv()
+        for c in range(chunks):
+            at = slice((part * chunks + c) * half, (part * chunks + c + 1) * half)
+            own_d[at] = own_d[at] + mid_d[part, c].astype(F32)
     own = [
         pltpu.make_async_copy(slope, own_gu_hbm, own_sem.at[0]),
         pltpu.make_async_copy(own_d, own_d_hbm, own_sem.at[1]),
@@ -386,45 +422,53 @@
     for copy in own:
         copy.start()
 
-    back_r[0:CAP] = back_s[0:CAP]
-    remote(back_s.at[sent], back_r.at[sent], back_ss, back_rs, (me, z)).wait_recv()
-
-    def combine(n, _):
-        cols = pl.ds(pl.multiple_of(n * COLS, COLS), COLS)
-        both = pick[0] + pick[1]
-        dtok_ref[:, cols] = dot(both, back_r[:, cols], NN).astype(BF16)
-        return 0
-
-    lax.fori_loop(0, chunks, combine, 0)
+    back_r[:, 0:CAP] = back_s[:, 0:CAP]
+    prob_r[0:CAP] = prob_s[0:CAP]
+    remote(prob_s.at[sent], prob_r.at[sent], prob_ss, prob_rs, (me, z)).wait_recv()
     for k in range(2):
-        terms = dot(pick[k], back_r[:, width : width + 128], NN).T
+        terms = dot(pick[k], prob_r[...], NN).T
         dprob_ref[k : k + 1] = (
             jnp.sum(terms, axis=0, keepdims=True) / probs_ref[...].astype(F32)[k : k + 1]
         )
 
+    def combine(n, _):
+        remote(
+            back_s.at[n, sent], back_r.at[n, sent], back_ss, back_rs.at[n], (me, z)
+        ).wait_recv()
+        cols = pl.ds(pl.multiple_of(n * COLS, COLS), COLS)
+        both = pick[0] + pick[1]
+        dtok_ref[:, cols] = dot(both, back_r[n], NN).astype(BF16)
+        return 0
+
+    lax.fori_loop(0, chunks, combine, 0)
+
+    for k in range(6):
+        for j in range(last + 1):
+            if k >= 4:
+                down_copy(k, j).wait_recv()
+            down_copy(k, j).wait_send()
+
     def finish(c, _):
         for k in range(6):
-            if k >= 2:
-                down_copy(k, c).wait_recv()
+            if k >= 4:
                 gate_up_copy(k, c)[1].wait_recv()
-            down_copy(k, c).wait_send()
             gate_up_copy(k, c)[1].wait_send()
         return 0
 
     lax.fori_loop(0, chunks, finish, 0)
     for copy in own:
         copy.wait()
-    remote(back_s.at[sent], back_r.at[sent], back_ss, back_rs, (me, z)).wait_send()
+    remote(
+        back_s.at[:, sent], back_r.at[:, sent], back_ss, back_rs.at[0], (me, z)
+    ).wait_send()
+    remote(prob_s.at[sent], prob_r.at[sent], prob_ss, prob_rs, (me, z)).wait_send()
 
 
 def add_up(own_gu, own_d, near_gu, near_d, tok_in, prob_in, tok, prob, gg, gu, gd):
     half = gg.shape[0]
-    total = near_gu[0, 0, 0].astype(F32) + near_gu[1, 0, 0].astype(F32)
-    gg[...] = own_gu[:, 0:COLS] + total[0:half]
-    gu[...] = own_gu[:, COLS : 2 * COLS] + total[half : 2 * half]
-    gd[...] = (
-        own_d[...] + near_d[0, 0, 0].astype(F32) + near_d[1, 0, 0].astype(F32)
-    )
+    gg[...] = own_gu[:, 0:COLS] + near_gu[0, 0, 0:half].astype(F32)
+    gu[...] = own_gu[:, COLS : 2 * COLS] + near_gu[0, 0, half : 2 * half].astype(F32)
+    gd[...] = own_d[...] + near_d[0, 0].astype(F32)
     tok[...] = tok_in[...]
     prob[...] = prob_in[...]
 
@@ -446,8 +490,8 @@
             jax.ShapeDtypeStruct((2, n_tok), F32),
             jax.ShapeDtypeStruct((hidden, 2 * COLS), F32),
             jax.ShapeDtypeStruct((hidden, COLS), F32),
-            jax.ShapeDtypeStruct((2, 2, chunks, 2 * half, COLS), BF16),
-            jax.ShapeDtypeStruct((2, 2, chunks, half, COLS), BF16),
+            jax.ShapeDtypeStruct((2, chunks, 2 * half, COLS), BF16),
+            jax.ShapeDtypeStruct((2, chunks, half, COLS), BF16),
         ),
         in_specs=[vmem] * 4 + [hbm] * 3,
         out_specs=[vmem] * 2 + [hbm] * 4,
@@ -466,21 +510,27 @@
             pltpu.VMEM((hidden, slots), F32),
             pltpu.VMEM((hidden, slots), F32),
             pltpu.VMEM((hidden, COLS), F32),
-            pltpu.VMEM((slots, width + 128), BF16),
-            pltpu.VMEM((slots, width + 128), BF16),
+            pltpu.VMEM((chunks, slots, COLS), BF16),
+            pltpu.VMEM((chunks, slots, COLS), BF16),
+            pltpu.VMEM((slots, 128), BF16),
+            pltpu.VMEM((slots, 128), BF16),
+            pltpu.VMEM((2, chunks, 2 * half, COLS), BF16),
+            pltpu.VMEM((2, chunks, half, COLS), BF16),
             pltpu.VMEM((2, chunks, 2 * half, COLS), BF16),
             pltpu.VMEM((2, chunks, half, COLS), BF16),
             dma((1 + 2 * HALVES,)),
             dma,
             dma((len(SHIFTS) // GROUP,)),
             dma,
+            dma((len(PIECES),)),
+            dma,
             dma((chunks,)),
             dma,
             dma,
             dma((6, chunks)),
             dma((6, chunks)),
-            dma((6, chunks)),
-            dma((6, chunks)),
+            dma((6, len(PIECES))),
+            dma((6, len(PIECES))),
             dma((2,)),
         ],
         compiler_params=pltpu.CompilerParams(
@@ -507,8 +557,8 @@
         in_specs=[
             pl.BlockSpec((half, 2 * COLS), step),
             pl.BlockSpec((half, COLS), step),
-            pl.BlockSpec((2, 1, 1, 2 * half, COLS), lambda p, c: (0, p, c, 0, 0)),
-            pl.BlockSpec((2, 1, 1, half, COLS), lambda p, c: (0, p, c, 0, 0)),
+            pl.BlockSpec((1, 1, 2 * half, COLS), lambda p, c: (p, c, 0, 0)),
+            pl.BlockSpec((1, 1, half, COLS), lambda p, c: (p, c, 0, 0)),
             rows,
             row_probs,
         ],

time: 178 us -> 171 us (0.961)
  Pallas kernels: 177 us -> 169 us
    pallas_call x1, Pallas kernels: 168 us -> 161 us  [per_device(): pl.pallas_call(kernel, out_shape=(jax.ShapeDtypeStruct((n_tok, width), BF...]
where the time goes in v4:
time: 171 us; the launch traced here: 170 us
  Pallas kernels  169 us (99%)
    pallas_call x1, Pallas kernels, per_device(): pl.pallas_call(kernel, out_shape=(jax.ShapeDtypeStruct((n_tok, width), BF...  161 us
    pallas_call x1, Pallas kernels, per_device(): pl.pallas_call(add_up, grid=(2, chunks), out_shape=(jax.ShapeDtypeStruct(...  7.95 us

profile of v4, /device:TPU:4, one launch (start us, length us, event | category | flops | bytes accessed | tf_op | source)
XLA Modules:
  0.0 170.2 jit_solution(464640567360105105)
XLA Ops:
  0.6 161.4 %routed_backward.1 = (bf16[256,2048]{1,0:T(8,128)(2,1)}, f32[2,256]{1,0:T(2,128)}, f32[768,1024]{1,0:T(8,128)}, f32[768,512]{1,0:T(8,128)}, bf16[2,4,192,512]{3,...) custom-call(bf16[256,2048]{1,0:T(8,128)(2,1)} %tok_ref.1, bf16[256,2048]{1,0:T(8,128)(2,1)} %dy_ref.1, s32[2,256]{1,0:T(2,128)} %bitcast.12, ...), custom_call_target="tpu_custom_call" | custom-call | tf_op jit(solution)/shard_map/routed_backward/pallas_call | solution.py:486
  162.1 7.9 %add_up.1 = (bf16[256,2048]{1,0:T(8,128)(2,1)}, f32[2,256]{1,0:T(2,128)}, f32[192,2048]{1,0:T(8,128)}, f32[192,2048]{1,0:T(8,128)}, f32[192,2048]{1,0:T(8,128)}) custom-call(f32[768,1024]{1,0:T(8,128)} %get-tuple-element.16.own_gu, f32[768,512]{1,0:T(8,128)} %get-tuple-element.17.own_d, bf16[2,4,192,512]{3,2,1,0:T(8,128)(2,1)} %get-tuple-element.18.near_gu, ...), custom_call_target="tpu_custom_call" | custom-call | tf_op jit(solution)/shard_map/add_up/pallas_call | solution.py:547

commit v5 on v4

--- a/solution.py
+++ b/solution.py
@@ -37,18 +37,20 @@
 
 def kernel(
     tok_ref,
-    dy_ref,
+    dy_hbm,
     routes_ref,
     probs_ref,
     wg_hbm,
     wu_hbm,
     wd_hbm,
-    dtok_ref,
+    dtok_hbm,
     dprob_ref,
     own_gu_hbm,
     own_d_hbm,
     near_gu,
     near_d,
+    dy_ref,
+    dtok_ref,
     pick,
     pick_scaled,
     xs,
@@ -85,6 +87,8 @@
     d_s,
     d_r,
     own_sem,
+    dy_sem,
+    dtok_sem,
 ):
     me, z = lax.axis_index("expert"), lax.axis_index("dp")
     cx, cy, core = me // 8, (me // 2) % 4, me % 2
@@ -119,6 +123,8 @@
     for other in (up, down):
         pl.semaphore_signal(barrier, inc=1, device_id=(me, other), device_id_type=MESH)
 
+    dy_load = pltpu.make_async_copy(dy_hbm, dy_ref, dy_sem)
+    dy_load.start()
     loads = [
         pltpu.make_async_copy(wd_hbm, wd, w_sem.at[0]),
     ]
@@ -149,34 +155,37 @@
         > lax.broadcasted_iota(jnp.int32, (n_tok, n_tok), 1)
     )
     earlier = jnp.where(earlier, 1.0, 0.0).astype(BF16)
-    slot = lax.broadcasted_iota(jnp.int32, (n_tok, n_shift * CAP), 1)
+    slot = lax.broadcasted_iota(jnp.int32, (n_tok, ROWS), 1)
     offset = place.astype(F32)
-    scaled = jnp.zeros((n_tok, n_shift * CAP), F32)
+    targets = []
     for k in range(2):
         named = lane == table[:, k : k + 1].astype(jnp.int32)
         hot = jnp.where(named, 1.0, 0.0)
         rank = dot(earlier, hot.astype(BF16), NN) + offset
         offset = offset + jnp.sum(hot, axis=0, keepdims=True)
         target = jnp.sum(jnp.where(named, rank, 0.0), axis=1, keepdims=True)
-        chosen = slot == target.astype(jnp.int32)
-        pick[k] = jnp.where(chosen, 1.0, 0.0).astype(BF16)
-        scaled = scaled + jnp.where(chosen, table[:, 2 + k : 3 + k], 0.0)
-    pick_scaled[...] = scaled.astype(BF16)
+        targets.append(target.astype(jnp.int32))
 
     for g in range(groups):
         at = slice(g * ROWS, (g + 1) * ROWS)
-        both = pick[0, :, at] + pick[1, :, at]
+        chosen = [slot == target - g * ROWS for target in targets]
+        both = jnp.where(chosen[0] | chosen[1], 1.0, 0.0).astype(BF16)
         for c in range(chunks):
             cols = slice(c * COLS, (c + 1) * COLS)
             xs[c, at] = dot(both, tok_ref[:, cols], TN).astype(BF16)
-        if g == 0:
-            pl.semaphore_wait(barrier, n_shift + 1)
-        for c in range(chunks):
+            if g == 0 and c == 0:
+                pl.semaphore_wait(barrier, n_shift + 1)
             for i in range(max(1, g * GROUP), (g + 1) * GROUP):
                 rows = slice(i * CAP, (i + 1) * CAP)
                 remote(
                     xs.at[c, rows], xr.at[c, rows], x_s, x_r.at[g], (owner(i), z)
                 ).start()
+        scaled = jnp.zeros((n_tok, ROWS), F32)
+        for k in range(2):
+            pick[k, :, at] = jnp.where(chosen[k], 1.0, 0.0).astype(BF16)
+            scaled = scaled + jnp.where(chosen[k], table[:, 2 + k : 3 + k], 0.0)
+        pick_scaled[:, at] = scaled.astype(BF16)
+    dy_load.wait()
     for c in range(chunks):
         cols = slice(c * COLS, (c + 1) * COLS)
         for g in range(groups):
@@ -431,13 +440,17 @@
             jnp.sum(terms, axis=0, keepdims=True) / probs_ref[...].astype(F32)[k : k + 1]
         )
 
+    def token_copy(n):
+        cols = pl.ds(pl.multiple_of(n * COLS, COLS), COLS)
+        return pltpu.make_async_copy(dtok_ref.at[n], dtok_hbm.at[:, cols], dtok_sem.at[n])
+
     def combine(n, _):
         remote(
             back_s.at[n, sent], back_r.at[n, sent], back_ss, back_rs.at[n], (me, z)
         ).wait_recv()
-        cols = pl.ds(pl.multiple_of(n * COLS, COLS), COLS)
         both = pick[0] + pick[1]
-        dtok_ref[:, cols] = dot(both, back_r[n], NN).astype(BF16)
+        dtok_ref[n] = dot(both, back_r[n], NN).astype(BF16)
+        token_copy(n).start()
         return 0
 
     lax.fori_loop(0, chunks, combine, 0)
@@ -449,6 +462,7 @@
             down_copy(k, j).wait_send()
 
     def finish(c, _):
+        token_copy(c).wait()
         for k in range(6):
             if k >= 4:
                 gate_up_copy(k, c)[1].wait_recv()
@@ -464,13 +478,63 @@
     remote(prob_s.at[sent], prob_r.at[sent], prob_ss, prob_rs, (me, z)).wait_send()
 
 
-def add_up(own_gu, own_d, near_gu, near_d, tok_in, prob_in, tok, prob, gg, gu, gd):
-    half = gg.shape[0]
-    gg[...] = own_gu[:, 0:COLS] + near_gu[0, 0, 0:half].astype(F32)
-    gu[...] = own_gu[:, COLS : 2 * COLS] + near_gu[0, 0, half : 2 * half].astype(F32)
-    gd[...] = own_d[...] + near_d[0, 0].astype(F32)
-    tok[...] = tok_in[...]
-    prob[...] = prob_in[...]
+def add_up(
+    own_gu_hbm,
+    own_d_hbm,
+    near_gu_hbm,
+    near_d_hbm,
+    tok_in,
+    prob_in,
+    tok_out,
+    prob_out,
+    gg_hbm,
+    gu_hbm,
+    gd_hbm,
+    own_gu,
+    own_d,
+    near_gu,
+    near_d,
+    sums,
+    in_sem,
+    out_sem,
+    tok_sem,
+):
+    half = own_gu.shape[1]
+    tiles = own_gu.shape[0]
+    chunks = tiles // 2
+    pairs = (
+        (own_gu_hbm, own_gu),
+        (own_d_hbm, own_d),
+        (near_gu_hbm, near_gu),
+        (near_d_hbm, near_d),
+    )
+    loads = []
+    for t in range(tiles):
+        rows = slice(t * half, (t + 1) * half)
+        for j, (src, dst) in enumerate(pairs):
+            part = src.at[rows] if j < 2 else src.at[t // chunks, t % chunks]
+            loads.append(pltpu.make_async_copy(part, dst.at[t], in_sem.at[t, j]))
+    for load in loads:
+        load.start()
+    tok = pltpu.make_async_copy(tok_in, tok_out, tok_sem)
+    tok.start()
+    prob_out[...] = prob_in[...]
+    stores = []
+    for t in range(tiles):
+        for load in loads[4 * t : 4 * t + 4]:
+            load.wait()
+        sums[t, 0] = own_gu[t, :, 0:COLS] + near_gu[t, 0:half].astype(F32)
+        sums[t, 1] = own_gu[t, :, COLS : 2 * COLS] + near_gu[t, half : 2 * half].astype(F32)
+        sums[t, 2] = own_d[t] + near_d[t].astype(F32)
+        low = slice((t // chunks) * half, (t // chunks + 1) * half)
+        cols = slice((t % chunks) * COLS, (t % chunks + 1) * COLS)
+        for j, out in enumerate((gg_hbm, gu_hbm, gd_hbm)):
+            store = pltpu.make_async_copy(sums.at[t, j], out.at[low, cols], out_sem.at[t, j])
+            store.start()
+            stores.append(store)
+    for store in stores:
+        store.wait()
+    tok.wait()
 
 
 def per_device(tokens, grad_out, routes, gate_probs, w_gate, w_up, w_down):
@@ -493,9 +557,11 @@
             jax.ShapeDtypeStruct((2, chunks, 2 * half, COLS), BF16),
             jax.ShapeDtypeStruct((2, chunks, half, COLS), BF16),
         ),
-        in_specs=[vmem] * 4 + [hbm] * 3,
-        out_specs=[vmem] * 2 + [hbm] * 4,
+        in_specs=[vmem, hbm, vmem, vmem] + [hbm] * 3,
+        out_specs=[hbm, vmem] + [hbm] * 4,
         scratch_shapes=[
+            pltpu.VMEM((n_tok, width), BF16),
+            pltpu.VMEM((chunks, n_tok, COLS), BF16),
             pltpu.VMEM((2, n_tok, slots), BF16),
             pltpu.VMEM((n_tok, slots), BF16),
             pltpu.VMEM((chunks, slots, COLS), BF16),
@@ -532,21 +598,18 @@
             dma((6, len(PIECES))),
             dma((6, len(PIECES))),
             dma((2,)),
+            dma,
+            dma((chunks,)),
         ],
         compiler_params=pltpu.CompilerParams(
             collective_id=0, has_side_effects=True, vmem_limit_bytes=63 << 20
         ),
         name="routed_backward",
     )(tokens, grad_out, routes.T, gate_probs.T, *weights)
-    step = lambda p, c: (p * chunks + c, 0)
-    fixed = lambda p, c: (0, 0)
-    tile = pl.BlockSpec((half, COLS), lambda p, c: (p, c))
-    rows = pl.BlockSpec((n_tok // HALVES, width), step)
-    row_probs = pl.BlockSpec((2, n_tok), fixed)
+    tiles = 2 * chunks
     shard = jax.ShapeDtypeStruct((hidden // 4, width), F32)
     d_tokens, d_probs, grad_g, grad_u, grad_d = pl.pallas_call(
         add_up,
-        grid=(2, chunks),
         out_shape=(
             jax.ShapeDtypeStruct((n_tok, width), BF16),
             jax.ShapeDtypeStruct((2, n_tok), F32),
@@ -554,15 +617,19 @@
             shard,
             shard,
         ),
-        in_specs=[
-            pl.BlockSpec((half, 2 * COLS), step),
-            pl.BlockSpec((half, COLS), step),
-            pl.BlockSpec((1, 1, 2 * half, COLS), lambda p, c: (p, c, 0, 0)),
-            pl.BlockSpec((1, 1, half, COLS), lambda p, c: (p, c, 0, 0)),
-            rows,
-            row_probs,
+        in_specs=[hbm] * 5 + [vmem],
+        out_specs=[hbm, vmem] + [hbm] * 3,
+        scratch_shapes=[
+            pltpu.VMEM((tiles, half, 2 * COLS), F32),
+            pltpu.VMEM((tiles, half, COLS), F32),
+            pltpu.VMEM((tiles, 2 * half, COLS), BF16),
+            pltpu.VMEM((tiles, half, COLS), BF16),
+            pltpu.VMEM((tiles, 3, half, COLS), F32),
+            dma((tiles, 4)),
+            dma((tiles, 3)),
+            dma,
         ],
-        out_specs=[rows, row_probs, tile, tile, tile],
+        compiler_params=pltpu.CompilerParams(vmem_limit_bytes=62 << 20),
         name="add_up",
     )(own_gu, own_d, near_gu, near_d, d_tokens, d_probs)
     return d_tokens, d_probs.T, grad_g[None], grad_u[None], grad_d[None]

time: 171 us -> 199 us (1.16)
  Pallas kernels: 169 us -> 198 us
    pallas_call x1, Pallas kernels: 7.95 us -> 34.6 us  [per_device(): pl.pallas_call(add_up, out_shape=(jax.ShapeDtypeStruct((n_tok, width), BF...]
where the time goes in v5:
time: 199 us
  Pallas kernels  198 us (99%)
    pallas_call x1, Pallas kernels, per_device(): pl.pallas_call(kernel, out_shape=(jax.ShapeDtypeStruct((n_tok, width), BF...  163 us
    pallas_call x1, Pallas kernels, per_device(): pl.pallas_call(add_up, out_shape=(jax.ShapeDtypeStruct((n_tok, width), BF...  34.6 us

profile of v5, /device:TPU:4, one launch (start us, length us, event | category | flops | bytes accessed | tf_op | source)
XLA Modules:
  0.0 198.6 jit_solution(14369239774810277165)
XLA Ops:
  0.6 163.1 %routed_backward.1 = (bf16[256,2048]{1,0:T(8,128)(2,1)}, f32[2,256]{1,0:T(2,128)}, f32[768,1024]{1,0:T(8,128)}, f32[768,512]{1,0:T(8,128)}, bf16[2,4,192,512]{3,...) custom-call(bf16[256,2048]{1,0:T(8,128)(2,1)} %tok_ref.1, bf16[256,2048]{1,0:T(8,128)(2,1)} %dy_hbm.1, s32[2,256]{1,0:T(2,128)} %bitcast.12, ...), custom_call_target="tpu_custom_call" | custom-call | tf_op jit(solution)/shard_map/routed_backward/pallas_call | solution.py:550
  163.7 34.6 %add_up.1 = (bf16[256,2048]{1,0:T(8,128)(2,1)}, f32[2,256]{1,0:T(2,128)}, f32[192,2048]{1,0:T(8,128)}, f32[192,2048]{1,0:T(8,128)}, f32[192,2048]{1,0:T(8,128)}) custom-call(f32[768,1024]{1,0:T(8,128)} %get-tuple-element.16.own_gu_hbm, f32[768,512]{1,0:T(8,128)} %get-tuple-element.17.own_d_hbm, bf16[2,4,192,512]{3,2,1,0:T(8,128)(2,1)} %get-tuple-element.18.near_gu_hbm, ...), custom_call_target="tpu_custom_call" | custom-call | tf_op jit(solution)/shard_map/add_up/pallas_call | solution.py:611

commit v6 on v5

--- a/solution.py
+++ b/solution.py
@@ -45,10 +45,8 @@
     wd_hbm,
     dtok_hbm,
     dprob_ref,
-    own_gu_hbm,
-    own_d_hbm,
-    near_gu,
-    near_d,
+    sum_gu_hbm,
+    sum_d_hbm,
     dy_ref,
     dtok_ref,
     pick,
@@ -73,6 +71,8 @@
     far_d,
     mid_gu,
     mid_d,
+    near_gu,
+    near_d,
     w_sem,
     x_s,
     x_r,
@@ -86,7 +86,7 @@
     gu_r,
     d_s,
     d_r,
-    own_sem,
+    sum_sem,
     dy_sem,
     dtok_sem,
 ):
@@ -424,13 +424,6 @@
         for c in range(chunks):
             at = slice((part * chunks + c) * half, (part * chunks + c + 1) * half)
             own_d[at] = own_d[at] + mid_d[part, c].astype(F32)
-    own = [
-        pltpu.make_async_copy(slope, own_gu_hbm, own_sem.at[0]),
-        pltpu.make_async_copy(own_d, own_d_hbm, own_sem.at[1]),
-    ]
-    for copy in own:
-        copy.start()
-
     back_r[:, 0:CAP] = back_s[:, 0:CAP]
     prob_r[0:CAP] = prob_s[0:CAP]
     remote(prob_s.at[sent], prob_r.at[sent], prob_ss, prob_rs, (me, z)).wait_recv()
@@ -453,36 +446,64 @@
         token_copy(n).start()
         return 0
 
-    lax.fori_loop(0, chunks, combine, 0)
-
+    def sum_copy(j, part, c):
+        src, dst = ((near_gu, sum_gu_hbm), (near_d, sum_d_hbm))[j]
+        return pltpu.make_async_copy(
+            src.at[part, c], dst.at[part, c], sum_sem.at[j, part, c]
+        )
+
+    def complete(c, _):
+        for part in range(2):
+            gate_up_copy(4 + part, c)[1].wait_recv()
+            rows = part_rows(part * chunks + c, half)
+            for j in range(2):
+                at = slice(j * half, (j + 1) * half)
+                value = slope[rows, j * COLS : (j + 1) * COLS]
+                near_gu[part, c, at] = (value + near_gu[part, c, at].astype(F32)).astype(BF16)
+            sum_copy(0, part, c).start()
+        return 0
+
+    def combine_and_complete(c, _):
+        combine(c, 0)
+        return complete(c, 0)
+
+    lax.fori_loop(0, chunks, combine_and_complete, 0)
+
+    for j in range(last + 1):
+        for part in range(2):
+            down_copy(4 + part, j).wait_recv()
+
+    def complete_down(c, _):
+        for part in range(2):
+            value = own_d[part_rows(part * chunks + c, half)]
+            near_d[part, c] = (value + near_d[part, c].astype(F32)).astype(BF16)
+            sum_copy(1, part, c).start()
+        return 0
+
+    lax.fori_loop(0, chunks, complete_down, 0)
     for k in range(6):
         for j in range(last + 1):
-            if k >= 4:
-                down_copy(k, j).wait_recv()
             down_copy(k, j).wait_send()
 
     def finish(c, _):
         token_copy(c).wait()
         for k in range(6):
-            if k >= 4:
-                gate_up_copy(k, c)[1].wait_recv()
             gate_up_copy(k, c)[1].wait_send()
+        for part in range(2):
+            for j in range(2):
+                sum_copy(j, part, c).wait()
         return 0
 
     lax.fori_loop(0, chunks, finish, 0)
-    for copy in own:
-        copy.wait()
     remote(
         back_s.at[:, sent], back_r.at[:, sent], back_ss, back_rs.at[0], (me, z)
     ).wait_send()
     remote(prob_s.at[sent], prob_r.at[sent], prob_ss, prob_rs, (me, z)).wait_send()
 
 
-def add_up(
-    own_gu_hbm,
-    own_d_hbm,
-    near_gu_hbm,
-    near_d_hbm,
+def widen(
+    sum_gu_hbm,
+    sum_d_hbm,
     tok_in,
     prob_in,
     tok_out,
@@ -490,51 +511,47 @@
     gg_hbm,
     gu_hbm,
     gd_hbm,
-    own_gu,
-    own_d,
-    near_gu,
-    near_d,
-    sums,
+    sum_gu,
+    sum_d,
+    tok,
+    wide,
     in_sem,
     out_sem,
     tok_sem,
 ):
-    half = own_gu.shape[1]
-    tiles = own_gu.shape[0]
-    chunks = tiles // 2
-    pairs = (
-        (own_gu_hbm, own_gu),
-        (own_d_hbm, own_d),
-        (near_gu_hbm, near_gu),
-        (near_d_hbm, near_d),
-    )
-    loads = []
-    for t in range(tiles):
-        rows = slice(t * half, (t + 1) * half)
-        for j, (src, dst) in enumerate(pairs):
-            part = src.at[rows] if j < 2 else src.at[t // chunks, t % chunks]
-            loads.append(pltpu.make_async_copy(part, dst.at[t], in_sem.at[t, j]))
-    for load in loads:
-        load.start()
-    tok = pltpu.make_async_copy(tok_in, tok_out, tok_sem)
-    tok.start()
+    parts, chunks, half = sum_d.shape[0:3]
+    tiles = [(p, c) for c in range(chunks) for p in range(parts)]
+    loads = {}
+    for t in tiles:
+        loads[t] = [
+            pltpu.make_async_copy(sum_gu_hbm.at[t], sum_gu.at[t], in_sem.at[t + (0,)]),
+            pltpu.make_async_copy(sum_d_hbm.at[t], sum_d.at[t], in_sem.at[t + (1,)]),
+        ]
+        for load in loads[t]:
+            load.start()
+    tok_load = pltpu.make_async_copy(tok_in, tok, tok_sem.at[0])
+    tok_load.start()
     prob_out[...] = prob_in[...]
     stores = []
-    for t in range(tiles):
-        for load in loads[4 * t : 4 * t + 4]:
+    for p, c in tiles:
+        for load in loads[p, c]:
             load.wait()
-        sums[t, 0] = own_gu[t, :, 0:COLS] + near_gu[t, 0:half].astype(F32)
-        sums[t, 1] = own_gu[t, :, COLS : 2 * COLS] + near_gu[t, half : 2 * half].astype(F32)
-        sums[t, 2] = own_d[t] + near_d[t].astype(F32)
-        low = slice((t // chunks) * half, (t // chunks + 1) * half)
-        cols = slice((t % chunks) * COLS, (t % chunks + 1) * COLS)
+        wide[p, c, 0] = sum_gu[p, c, 0:half].astype(F32)
+        wide[p, c, 1] = sum_gu[p, c, half : 2 * half].astype(F32)
+        wide[p, c, 2] = sum_d[p, c].astype(F32)
+        low = slice(p * half, (p + 1) * half)
+        cols = slice(c * COLS, (c + 1) * COLS)
         for j, out in enumerate((gg_hbm, gu_hbm, gd_hbm)):
-            store = pltpu.make_async_copy(sums.at[t, j], out.at[low, cols], out_sem.at[t, j])
+            store = pltpu.make_async_copy(
+                wide.at[p, c, j], out.at[low, cols], out_sem.at[p, c, j]
+            )
             store.start()
             stores.append(store)
+    tok_load.wait()
+    stores.append(pltpu.make_async_copy(tok, tok_out, tok_sem.at[1]))
+    stores[-1].start()
     for store in stores:
         store.wait()
-    tok.wait()
 
 
 def per_device(tokens, grad_out, routes, gate_probs, w_gate, w_up, w_down):
@@ -547,18 +564,16 @@
     hbm = pl.BlockSpec(memory_space=pl.ANY)
     weights = [w[0] for w in (w_gate, w_up, w_down)]
     dma = pltpu.SemaphoreType.DMA
-    d_tokens, d_probs, own_gu, own_d, near_gu, near_d = pl.pallas_call(
+    d_tokens, d_probs, sum_gu, sum_d = pl.pallas_call(
         kernel,
         out_shape=(
             jax.ShapeDtypeStruct((n_tok, width), BF16),
             jax.ShapeDtypeStruct((2, n_tok), F32),
-            jax.ShapeDtypeStruct((hidden, 2 * COLS), F32),
-            jax.ShapeDtypeStruct((hidden, COLS), F32),
             jax.ShapeDtypeStruct((2, chunks, 2 * half, COLS), BF16),
             jax.ShapeDtypeStruct((2, chunks, half, COLS), BF16),
         ),
         in_specs=[vmem, hbm, vmem, vmem] + [hbm] * 3,
-        out_specs=[hbm, vmem] + [hbm] * 4,
+        out_specs=[hbm, vmem, hbm, hbm],
         scratch_shapes=[
             pltpu.VMEM((n_tok, width), BF16),
             pltpu.VMEM((chunks, n_tok, COLS), BF16),
@@ -584,6 +599,8 @@
             pltpu.VMEM((2, chunks, half, COLS), BF16),
             pltpu.VMEM((2, chunks, 2 * half, COLS), BF16),
             pltpu.VMEM((2, chunks, half, COLS), BF16),
+            pltpu.VMEM((2, chunks, 2 * half, COLS), BF16),
+            pltpu.VMEM((2, chunks, half, COLS), BF16),
             dma((1 + 2 * HALVES,)),
             dma,
             dma((len(SHIFTS) // GROUP,)),
@@ -597,7 +614,7 @@
             dma((6, chunks)),
             dma((6, len(PIECES))),
             dma((6, len(PIECES))),
-            dma((2,)),
+            dma((2, 2, chunks)),
             dma,
             dma((chunks,)),
         ],
@@ -606,10 +623,9 @@
         ),
         name="routed_backward",
     )(tokens, grad_out, routes.T, gate_probs.T, *weights)
-    tiles = 2 * chunks
     shard = jax.ShapeDtypeStruct((hidden // 4, width), F32)
     d_tokens, d_probs, grad_g, grad_u, grad_d = pl.pallas_call(
-        add_up,
+        widen,
         out_shape=(
             jax.ShapeDtypeStruct((n_tok, width), BF16),
             jax.ShapeDtypeStruct((2, n_tok), F32),
@@ -617,21 +633,20 @@
             shard,
             shard,
         ),
-        in_specs=[hbm] * 5 + [vmem],
+        in_specs=[hbm] * 3 + [vmem],
         out_specs=[hbm, vmem] + [hbm] * 3,
         scratch_shapes=[
-            pltpu.VMEM((tiles, half, 2 * COLS), F32),
-            pltpu.VMEM((tiles, half, COLS), F32),
-            pltpu.VMEM((tiles, 2 * half, COLS), BF16),
-            pltpu.VMEM((tiles, half, COLS), BF16),
-            pltpu.VMEM((tiles, 3, half, COLS), F32),
-            dma((tiles, 4)),
-            dma((tiles, 3)),
-            dma,
+            pltpu.VMEM((2, chunks, 2 * half, COLS), BF16),
+            pltpu.VMEM((2, chunks, half, COLS), BF16),
+            pltpu.VMEM((n_tok, width), BF16),
+            pltpu.VMEM((2, chunks, 3, half, COLS), F32),
+            dma((2, chunks, 2)),
+            dma((2, chunks, 3)),
+            dma((2,)),
         ],
         compiler_params=pltpu.CompilerParams(vmem_limit_bytes=62 << 20),
-        name="add_up",
-    )(own_gu, own_d, near_gu, near_d, d_tokens, d_probs)
+        name="widen",
+    )(sum_gu, sum_d, d_tokens, d_probs)
     return d_tokens, d_probs.T, grad_g[None], grad_u[None], grad_d[None]
 
 

time: 199 us -> 170 us (0.85)
  Pallas kernels: 198 us -> 169 us
    pallas_call x1, Pallas kernels: 34.6 us -> 5.16 us  [per_device(): pl.pallas_call(widen, out_shape=(jax.ShapeDtypeStruct((n_tok, width), BF1...]
where the time goes in v6:
time: 170 us
  Pallas kernels  169 us (99%)
    pallas_call x1, Pallas kernels, per_device(): pl.pallas_call(kernel, out_shape=(jax.ShapeDtypeStruct((n_tok, width), BF...  164 us
    pallas_call x1, Pallas kernels, per_device(): pl.pallas_call(widen, out_shape=(jax.ShapeDtypeStruct((n_tok, width), BF1...  5.16 us

profile of v6, /device:TPU:4, one launch (start us, length us, event | category | flops | bytes accessed | tf_op | source)
XLA Modules:
  0.0 169.7 jit_solution(3984411078931268785)
XLA Ops:
  0.6 163.7 %routed_backward.1 = (bf16[256,2048]{1,0:T(8,128)(2,1)}, f32[2,256]{1,0:T(2,128)}, bf16[2,4,192,512]{3,2,1,0:T(8,128)(2,1)}, bf16[2,4,96,512]{3,2,1,0:T(8,128)(2,1)}) custom-call(bf16[256,2048]{1,0:T(8,128)(2,1)} %tok_ref.1, bf16[256,2048]{1,0:T(8,128)(2,1)} %dy_hbm.1, s32[2,256]{1,0:T(2,128)} %bitcast.12, bf16[2,256]{1,0:T(2,128)(2,1)} %bitcast.13, ...), custom_call_target="tpu_custom_call" | custom-call | tf_op jit(solution)/shard_map/routed_backward/pallas_call | solution.py:567
  164.3 5.2 %widen.1 = (bf16[256,2048]{1,0:T(8,128)(2,1)}, f32[2,256]{1,0:T(2,128)}, f32[192,2048]{1,0:T(8,128)}, f32[192,2048]{1,0:T(8,128)}, f32[192,2048]{1,0:T(8,128)}) custom-call(bf16[2,4,192,512]{3,2,1,0:T(8,128)(2,1)} %get-tuple-element.14.sum_gu_hbm, bf16[2,4,96,512]{3,2,1,0:T(8,128)(2,1)} %get-tuple-element.15.sum_d_hbm, ...), custom_call_target="tpu_custom_call" | custom-call | tf_op jit(solution)/shard_map/widen/pallas_call | solution.py:627

commit v7 on v6

--- a/solution.py
+++ b/solution.py
@@ -24,6 +24,7 @@
     (dx, dy, dc) for ring in RINGS for dc in (0, 1) for dx, dy in ring
 ]
 CAP = 32
+PROB_ROWS = CAP // 2
 GROUP = 8
 ROWS = GROUP * CAP
 COLS = 512
@@ -36,7 +37,7 @@
 
 
 def kernel(
-    tok_ref,
+    tok_hbm,
     dy_hbm,
     routes_ref,
     probs_ref,
@@ -47,6 +48,7 @@
     dprob_ref,
     sum_gu_hbm,
     sum_d_hbm,
+    tok_ref,
     dy_ref,
     dtok_ref,
     pick,
@@ -87,6 +89,7 @@
     d_s,
     d_r,
     sum_sem,
+    tok_sem,
     dy_sem,
     dtok_sem,
 ):
@@ -123,8 +126,9 @@
     for other in (up, down):
         pl.semaphore_signal(barrier, inc=1, device_id=(me, other), device_id_type=MESH)
 
+    tok_load = pltpu.make_async_copy(tok_hbm, tok_ref, tok_sem)
+    tok_load.start()
     dy_load = pltpu.make_async_copy(dy_hbm, dy_ref, dy_sem)
-    dy_load.start()
     loads = [
         pltpu.make_async_copy(wd_hbm, wd, w_sem.at[0]),
     ]
@@ -137,8 +141,6 @@
                     w_sem.at[1 + 2 * h + j],
                 )
             )
-    for load in loads:
-        load.start()
 
     line = lax.broadcasted_iota(jnp.int32, (128, n_tok), 0)
     routes = routes_ref[...].astype(F32)
@@ -166,6 +168,7 @@
         target = jnp.sum(jnp.where(named, rank, 0.0), axis=1, keepdims=True)
         targets.append(target.astype(jnp.int32))
 
+    tok_load.wait()
     for g in range(groups):
         at = slice(g * ROWS, (g + 1) * ROWS)
         chosen = [slot == target - g * ROWS for target in targets]
@@ -180,6 +183,9 @@
                 remote(
                     xs.at[c, rows], xr.at[c, rows], x_s, x_r.at[g], (owner(i), z)
                 ).start()
+        if g == 0:
+            for load in [dy_load] + loads:
+                load.start()
         scaled = jnp.zeros((n_tok, ROWS), F32)
         for k in range(2):
             pick[k, :, at] = jnp.where(chosen[k], 1.0, 0.0).astype(BF16)
@@ -384,10 +390,15 @@
 
     high = total.astype(BF16).astype(F32)
     line = lax.broadcasted_iota(jnp.int32, (128, n_shift * CAP), 0)
-    pair = jnp.where(line == 0, high, jnp.where(line == 1, total - high, 0.0))
-    prob_s[...] = pair.T.astype(BF16)
+    upper = lax.broadcasted_iota(jnp.int32, (128, n_shift * CAP), 1) % CAP // PROB_ROWS
+    pair = jnp.where(line == 2 * upper, high, 0.0)
+    pair = jnp.where(line == 2 * upper + 1, total - high, pair)
+    pair = pair.T.reshape(n_shift, 2, PROB_ROWS, 128)
+    pair = (pair[:, 0] + pair[:, 1]).astype(BF16)
+    prob_s[...] = pair.reshape(n_shift * PROB_ROWS, 128)
+    prob_sent = slice(PROB_ROWS, n_shift * PROB_ROWS)
     for i in range(1, n_shift):
-        rows = slice(i * CAP, (i + 1) * CAP)
+        rows = slice(i * PROB_ROWS, (i + 1) * PROB_ROWS)
         remote(
             prob_s.at[rows], prob_r.at[rows], prob_ss, prob_rs, (source(i), z)
         ).start()
@@ -425,12 +436,20 @@
             at = slice((part * chunks + c) * half, (part * chunks + c + 1) * half)
             own_d[at] = own_d[at] + mid_d[part, c].astype(F32)
     back_r[:, 0:CAP] = back_s[:, 0:CAP]
-    prob_r[0:CAP] = prob_s[0:CAP]
-    remote(prob_s.at[sent], prob_r.at[sent], prob_ss, prob_rs, (me, z)).wait_recv()
+    prob_r[0:PROB_ROWS] = prob_s[0:PROB_ROWS]
+    remote(
+        prob_s.at[prob_sent], prob_r.at[prob_sent], prob_ss, prob_rs, (me, z)
+    ).wait_recv()
+    terms = prob_r[...].astype(F32).reshape(n_shift, PROB_ROWS, 128)
+    column = lax.broadcasted_iota(jnp.int32, terms.shape, 2)
+    terms = jnp.stack(
+        [jnp.where(column < 2, terms, 0.0), jnp.where(column >= 2, terms, 0.0)], axis=1
+    )
+    terms = terms.reshape(n_shift * CAP, 128).astype(BF16)
     for k in range(2):
-        terms = dot(pick[k], prob_r[...], NN).T
+        mine = dot(pick[k], terms, NN).T
         dprob_ref[k : k + 1] = (
-            jnp.sum(terms, axis=0, keepdims=True) / probs_ref[...].astype(F32)[k : k + 1]
+            jnp.sum(mine, axis=0, keepdims=True) / probs_ref[...].astype(F32)[k : k + 1]
         )
 
     def token_copy(n):
@@ -498,7 +517,9 @@
     remote(
         back_s.at[:, sent], back_r.at[:, sent], back_ss, back_rs.at[0], (me, z)
     ).wait_send()
-    remote(prob_s.at[sent], prob_r.at[sent], prob_ss, prob_rs, (me, z)).wait_send()
+    remote(
+        prob_s.at[prob_sent], prob_r.at[prob_sent], prob_ss, prob_rs, (me, z)
+    ).wait_send()
 
 
 def widen(
@@ -572,9 +593,10 @@
             jax.ShapeDtypeStruct((2, chunks, 2 * half, COLS), BF16),
             jax.ShapeDtypeStruct((2, chunks, half, COLS), BF16),
         ),
-        in_specs=[vmem, hbm, vmem, vmem] + [hbm] * 3,
+        in_specs=[hbm, hbm, vmem, vmem] + [hbm] * 3,
         out_specs=[hbm, vmem, hbm, hbm],
         scratch_shapes=[
+            pltpu.VMEM((n_tok, width), BF16),
             pltpu.VMEM((n_tok, width), BF16),
             pltpu.VMEM((chunks, n_tok, COLS), BF16),
             pltpu.VMEM((2, n_tok, slots), BF16),
@@ -593,8 +615,8 @@
             pltpu.VMEM((hidden, COLS), F32),
             pltpu.VMEM((chunks, slots, COLS), BF16),
             pltpu.VMEM((chunks, slots, COLS), BF16),
-            pltpu.VMEM((slots, 128), BF16),
-            pltpu.VMEM((slots, 128), BF16),
+            pltpu.VMEM((slots // 2, 128), BF16),
+            pltpu.VMEM((slots // 2, 128), BF16),
             pltpu.VMEM((2, chunks, 2 * half, COLS), BF16),
             pltpu.VMEM((2, chunks, half, COLS), BF16),
             pltpu.VMEM((2, chunks, 2 * half, COLS), BF16),
@@ -615,6 +637,7 @@
             dma((6, len(PIECES))),
             dma((6, len(PIECES))),
             dma((2, 2, chunks)),
+            dma,
             dma,
             dma((chunks,)),
         ],

time: 170 us -> 169 us (level)
  no operation moved by 1% of the time
where the time goes in v7:
time: 169 us
  Pallas kernels  168 us (99%)
    pallas_call x1, Pallas kernels, per_device(): pl.pallas_call(kernel, out_shape=(jax.ShapeDtypeStruct((n_tok, width), BF...  163 us
    pallas_call x1, Pallas kernels, per_device(): pl.pallas_call(widen, out_shape=(jax.ShapeDtypeStruct((n_tok, width), BF1...  5.16 us

profile of v7, /device:TPU:4, one launch (start us, length us, event | category | flops | bytes accessed | tf_op | source)
XLA Modules:
  0.0 169.1 jit_solution(16262014202718878826)
XLA Ops:
  0.6 163.1 %routed_backward.1 = (bf16[256,2048]{1,0:T(8,128)(2,1)}, f32[2,256]{1,0:T(2,128)}, bf16[2,4,192,512]{3,2,1,0:T(8,128)(2,1)}, bf16[2,4,96,512]{3,2,1,0:T(8,128)(2,1)}) custom-call(bf16[256,2048]{1,0:T(8,128)(2,1)} %tok_hbm.1, bf16[256,2048]{1,0:T(8,128)(2,1)} %dy_hbm.1, s32[2,256]{1,0:T(2,128)} %bitcast.12, bf16[2,256]{1,0:T(2,128)(2,1)} %bitcast.13, ...), custom_call_target="tpu_custom_call" | custom-call | tf_op jit(solution)/shard_map/routed_backward/pallas_call | solution.py:588
  163.8 5.2 %widen.1 = (bf16[256,2048]{1,0:T(8,128)(2,1)}, f32[2,256]{1,0:T(2,128)}, f32[192,2048]{1,0:T(8,128)}, f32[192,2048]{1,0:T(8,128)}, f32[192,2048]{1,0:T(8,128)}) custom-call(bf16[2,4,192,512]{3,2,1,0:T(8,128)(2,1)} %get-tuple-element.14.sum_gu_hbm, bf16[2,4,96,512]{3,2,1,0:T(8,128)(2,1)} %get-tuple-element.15.sum_d_hbm, ...), custom_call_target="tpu_custom_call" | custom-call | tf_op jit(solution)/shard_map/widen/pallas_call | solution.py:650

commit v8 on v7

--- a/solution.py
+++ b/solution.py
@@ -369,21 +369,20 @@
     )
 
     def with_far(n, _):
-        return_tile(0, n)
-
         @pl.when(n < chunks - 1)
         def _():
             send_gate_up(0, n + 1)
             send_gate_up(1, n + 1)
 
+        return_tile(0, n)
         return 0
 
     lax.fori_loop(0, chunks, with_far, 0)
 
     def with_near(n, _):
-        return_tile(1, n)
         send_gate_up(2, n)
         send_gate_up(3, n)
+        return_tile(1, n)
         return 0
 
     lax.fori_loop(0, chunks, with_near, 0)

time: 169 us -> 169 us (level)
  no operation moved by 1% of the time
where the time goes in v8:
time: 169 us
  Pallas kernels  168 us (99%)
    pallas_call x1, Pallas kernels, per_device(): pl.pallas_call(kernel, out_shape=(jax.ShapeDtypeStruct((n_tok, width), BF...  163 us
    pallas_call x1, Pallas kernels, per_device(): pl.pallas_call(widen, out_shape=(jax.ShapeDtypeStruct((n_tok, width), BF1...  5.16 us

profile of v8, /device:TPU:4, one launch (start us, length us, event | category | flops | bytes accessed | tf_op | source)
XLA Modules:
  0.0 169.1 jit_solution(14866650877646645530)
XLA Ops:
  0.6 163.1 %routed_backward.1 = (bf16[256,2048]{1,0:T(8,128)(2,1)}, f32[2,256]{1,0:T(2,128)}, bf16[2,4,192,512]{3,2,1,0:T(8,128)(2,1)}, bf16[2,4,96,512]{3,2,1,0:T(8,128)(2,1)}) custom-call(bf16[256,2048]{1,0:T(8,128)(2,1)} %tok_hbm.1, bf16[256,2048]{1,0:T(8,128)(2,1)} %dy_hbm.1, s32[2,256]{1,0:T(2,128)} %bitcast.12, bf16[2,256]{1,0:T(2,128)(2,1)} %bitcast.13, ...), custom_call_target="tpu_custom_call" | custom-call | tf_op jit(solution)/shard_map/routed_backward/pallas_call | solution.py:587
  163.8 5.2 %widen.1 = (bf16[256,2048]{1,0:T(8,128)(2,1)}, f32[2,256]{1,0:T(2,128)}, f32[192,2048]{1,0:T(8,128)}, f32[192,2048]{1,0:T(8,128)}, f32[192,2048]{1,0:T(8,128)}) custom-call(bf16[2,4,192,512]{3,2,1,0:T(8,128)(2,1)} %get-tuple-element.14.sum_gu_hbm, bf16[2,4,96,512]{3,2,1,0:T(8,128)(2,1)} %get-tuple-element.15.sum_d_hbm, ...), custom_call_target="tpu_custom_call" | custom-call | tf_op jit(solution)/shard_map/widen/pallas_call | solution.py:649
